TPU v7x, 128 devices: a whole 4x4x4 slice. The times are simulated.
128 devices in a mesh: ref: 2 (over core), lines: 8 (over y, z_hi), cells: 8 (over z_lo, x).
Axes of the slice: x: 4, y: 4, z: 4 (z_hi: 2, z_lo: 2; z = z_hi * 2 + z_lo), core: 2. Of those that a mesh axis runs over, the one named last changes fastest.
Arguments:
- sens: bfloat16 [32768, 128, 128], P(('lines', 'cells')), may hold values from -0.125 to 0.125
- block_rows: int32 [32768], P(('lines', 'cells')), may hold values from 0 to 31
- block_cols: int32 [32768], P(('lines', 'cells')), may hold values from 0 to 2047, as said below
- neighbours: int32 [6, 262144], P(None, ('lines', 'cells')), may hold values from 0 to 262143, as said below
- observed: float32 [262144], P(('lines', 'cells')), may hold values from -6 to 6
- data_weight: float32 [262144], P(('lines', 'cells')), may hold values from 0.3 to 5.2
- smallness: float32 [262144], P(('lines', 'cells')), may hold values from 0.1 to 1
- model: float32 [524288], P(('ref', 'lines', 'cells')), parts along dimension 0, may hold values from -6 to 6
- reference_model: float32 [524288], P(('ref', 'lines', 'cells')), parts along dimension 0, may hold values from -6 to 6
Outputs:
- update: float32 [524288], P(('ref', 'lines', 'cells')), parts along dimension 0
- cg_residual: float32 [524288], P(('ref', 'lines', 'cells')), parts along dimension 0
There are 2 independent parts, one for each index of `ref`. A program takes and returns all parts, laid end to end along the dimension named above; an argument that names none is the same for every part. Nothing has to cross between parts.
Inputs may be any that keep to these rules, and one draw needn't show every extreme that they name: `block_cols`: devices hold aligned runs of 512 blocks; cell block c is owned by device c // 32. The blocks of one device name at most 16 cell blocks of any one owner, and in every draw one owner gets exactly 16 from every device. `neighbours`: A cell's own index stands for a missing neighbour; the relation is symmetric, and every neighbour lies within 1024 cells of its cell, some exactly that far.
All inputs are finite; a program needn't handle non-finite values.
Results may differ from a plain program's by a relative error of at most 0.0131.
Values may be sent and summed in bfloat16 or wider, within the bound.
No kernel may reach another device: no remote copies, remote signals or barrier semaphores. Data moves between devices by JAX's collectives and lax.ppermute only.
A program may use at most 64 MiB of HBM per device.

v0:
```python
import jax
import jax.numpy as jnp
from jax import lax
from jax.sharding import PartitionSpec as P

CG_STEPS = 3


beta_reg = 0.5


def padded_2(cells, sides, width):
    for axis, dim in sides:
        count = lax.axis_size(axis)
        ends = count - 1
        head = lax.slice_in_dim(cells, 0, width, axis=dim)
        tail = lax.slice_in_dim(cells, cells.shape[dim] - width, cells.shape[dim], axis=dim)
        cells = jnp.concatenate(
            [
                lax.ppermute(tail, axis, [(i, (i + 1) % count) for i in range(ends)]),
                cells,
                lax.ppermute(head, axis, [((i + 1) % count, i) for i in range(ends)]),
            ],
            axis=dim,
        )
    return cells


def per_device(
    sens,
    block_rows,
    block_cols,
    neighbours,
    observed,
    data_weight,
    smallness,
    model,
    reference_model,
):
    row_blocks = observed.shape[0] // 128
    own_cells = model.shape[0]
    col_blocks = own_cells // 128
    devices = lax.axis_size(("lines", "cells"))
    offset = lax.axis_index(("lines", "cells")) * own_cells
    margin = own_cells // 4
    local_index = neighbours - offset + margin
    row_pick = (block_rows[None, :] == jnp.arange(row_blocks, dtype=jnp.int32)[:, None]).astype(
        jnp.float32
    )
    weight_sq = data_weight * data_weight

    def forward(vector):
        gathered = lax.all_gather(vector, ("lines", "cells"), axis=0, tiled=True)
        columns = gathered.reshape(-1, 128)[block_cols]
        products = jnp.einsum("bij,bj->bi", sens, columns, preferred_element_type=jnp.float32)
        return jnp.dot(
            row_pick, products, precision=lax.Precision.HIGHEST, preferred_element_type=jnp.float32
        ).reshape(-1)

    def backward(weighted):
        picked = weighted.reshape(row_blocks, 128)[block_rows]
        partial_terms = jnp.einsum("bij,bi->bj", sens, picked, preferred_element_type=jnp.float32)
        spread = (
            jnp.zeros((col_blocks * devices, 128), jnp.float32).at[block_cols].add(partial_terms)
        )
        return lax.psum_scatter(
            spread.reshape(-1), ("lines", "cells"), scatter_dimension=0, tiled=True
        )

    def smooth(vector):
        padded = padded_2(vector, ((("lines", "cells"), 0),), margin)
        nearby = padded[local_index]
        return (smallness + 6.0) * vector - jnp.sum(nearby, axis=0)

    def squares(residual):
        return lax.psum(jnp.sum(residual * residual), ("lines", "cells"))

    misfit = (weight_sq * (forward(model.astype(jnp.bfloat16)) - observed)).astype(jnp.bfloat16)
    right_side = -(backward(misfit) + beta_reg * smooth(model - reference_model))
    update = jnp.zeros_like(right_side)
    residual = right_side
    direction = right_side
    norm_now = squares(residual)
    for iteration in range(CG_STEPS):
        direction_half = direction.astype(jnp.bfloat16)
        predicted = forward(direction_half)
        weighted = (weight_sq * predicted).astype(jnp.bfloat16)
        bent = smooth(direction)
        transposed = backward(weighted)
        curvature = lax.psum(
            jnp.sum(direction_half.astype(jnp.float32) * transposed)
            + beta_reg * jnp.sum(direction * bent),
            ("lines", "cells"),
        )
        image = transposed + beta_reg * bent
        alpha = norm_now / curvature
        update = update + alpha * direction
        residual = residual - alpha * image
        norm_next = squares(residual)
        direction = residual + norm_next / norm_now * direction
        norm_now = norm_next
    return (update, residual)


def solution(mesh):
    in_specs = (
        P(("lines", "cells"), None, None),
        P(("lines", "cells")),
        P(("lines", "cells")),
        P(None, ("lines", "cells")),
        P(("lines", "cells")),
        P(("lines", "cells")),
        P(("lines", "cells")),
        P(("ref", "lines", "cells")),
        P(("ref", "lines", "cells")),
    )
    out_specs = (P(("ref", "lines", "cells")), P(("ref", "lines", "cells")))
    return jax.shard_map(
        per_device, mesh=mesh, in_specs=in_specs, out_specs=out_specs, check_vma=False
    )
```

profile of v0, /device:TPU:0, one launch (start us, length us, event | category | flops | bytes accessed | tf_op | source)
XLA Modules:
  0.0 2408.6 jit_solution(5275958683108193666)
XLA Ops:
  9.3 4.5 collective-permute-start
  14.5 178.9 %all_gather.12 = bf16[262144]{0:T(1024)(128)(2,1)S(1)} all-gather(bf16[4096]{0:T(1024)(128)(2,1)S(1)} %get-tuple-element.25), channel_id=1, replica_groups=mesh['ref'=2,'lines'=8,'cells'=8] {'lines','cells'}, dimensions={0}, use_global_device_ids=true | all-gather | bytes 532480 | tf_op jit(solution)/shard_map/all_gather | solution.py:53
  194.2 1.3 gather_fusion
  195.6 12.2 fusion.35
  208.0 1.3 gather_fusion.1
  209.4 8.1 fusion.33
  217.5 3.3 scatter_custom_fusion
  222.3 135.5 %gather_fusion.2 = f32[24576]{0:T(1024)S(1)} fusion(f32[6144]{0:T(1024)S(1)} %pad_maximum_fusion, s32[24576]{0:T(1024)S(1)} %broadcast_clamp_fusion), kind=kCustom, calls=%fused_computation.2 | custom fusion | bytes 294912 | tf_op jit(solution)/shard_map/gather | solution.py:72
  358.7 1.3 collective-permute-start.3
  360.0 4.5 collective-permute-start.2
  364.5 1.3 collective-permute-done.2
  365.8 135.5 %gather_fusion.5 = f32[24576]{0:T(1024)S(1)} fusion(f32[6144]{0:T(1024)S(1)} %pad_maximum_fusion.1, s32[24576]{0:T(1024)S(1)} %broadcast_clamp_fusion), kind=kCustom, calls=%fused_computation.5 | custom fusion | bytes 294912 | tf_op jit(solution)/shard_map/gather | solution.py:72
  502.1 174.4 %all_gather.13 = bf16[262144]{0:T(1024)(128)(2,1)S(1)} all-gather(bf16[4096]{0:T(1024)(128)(2,1)S(1)} %get-tuple-element.22), channel_id=1, replica_groups=mesh['ref'=2,'lines'=8,'cells'=8] {'lines','cells'}, dimensions={0}, use_global_device_ids=true | all-gather | bytes 532480 | tf_op jit(solution)/shard_map/all_gather | solution.py:53
  676.5 1.3 gather_fusion.3
  677.8 12.2 fusion.31
  690.3 1.3 gather_fusion.4
  691.6 8.1 fusion.29
  699.7 3.3 scatter_custom_fusion.1
  703.7 122.6 %all-reduce.12.cloned.1.call-done = f32[262144]{0:T(1024)} async-done(((f32[262144]{0:T(1024)}), f32[262144]{0:T(1024)}) %all-reduce.12.cloned.1.call-update) | async-done | bytes 1048592
  826.3 1.3 multiply_reduce_fusion.7
  828.3 175.7 %all-reduce.4 = (f32[]{:T(128)}, f32[]{:T(128)}) all-reduce(f32[]{:T(128)} %get-tuple-element.3, f32[]{:T(128)S(6)} %add.111), channel_id=1, replica_groups=mesh['ref'=2,'lines'=8,'cells'=8] {'lines','cells'}, use_global_device_ids=true, to_apply=%region_4.0 | all-reduce | flops 2 | bytes 16 | tf_op jit(solution)/shard_map/psum | solution.py:76
  1005.4 1.3 multiply_reduce_fusion.5
  1006.7 172.4 %psum.44 = f32[]{:T(128)} all-reduce(f32[]{:T(128)} %get-tuple-element.12), channel_id=1, replica_groups=mesh['ref'=2,'lines'=8,'cells'=8] {'lines','cells'}, use_global_device_ids=true, to_apply=%region_12.0 | all-reduce | flops 1 | bytes 8 | tf_op jit(solution)/shard_map/psum | solution.py:76
  1180.4 174.1 %all_gather.14 = bf16[262144]{0:T(1024)(128)(2,1)S(1)} all-gather(bf16[4096]{0:T(1024)(128)(2,1)S(1)} %get-tuple-element.10), channel_id=1, replica_groups=mesh['ref'=2,'lines'=8,'cells'=8] {'lines','cells'}, dimensions={0}, use_global_device_ids=true | all-gather | bytes 532480 | tf_op jit(solution)/shard_map/all_gather | solution.py:53
  1354.6 1.3 gather_fusion.6
  1355.9 12.2 fusion.27
  1368.4 1.3 gather_fusion.7
  1369.7 8.1 fusion.25
  1377.8 3.3 scatter_custom_fusion.2
  1382.5 4.5 collective-permute-start.4
  1387.0 1.3 collective-permute-done.4
  1388.3 135.5 %gather_fusion.8 = f32[24576]{0:T(1024)S(1)} fusion(f32[6144]{0:T(1024)S(1)} %pad_maximum_fusion.2, s32[24576]{0:T(1024)S(1)} %broadcast_clamp_fusion), kind=kCustom, calls=%fused_computation.8 | custom fusion | bytes 294912 | tf_op jit(solution)/shard_map/gather | solution.py:72
  1525.2 1.3 multiply_reduce_fusion.4
  1527.2 174.5 %psum.45 = f32[]{:T(128)} all-reduce(f32[]{:T(128)S(6)} %add.114), channel_id=1, replica_groups=mesh['ref'=2,'lines'=8,'cells'=8] {'lines','cells'}, use_global_device_ids=true, to_apply=%region_18.0 | all-reduce | flops 1 | bytes 8 | tf_op jit(solution)/shard_map/psum | solution.py:90
  1703.1 1.3 multiply_reduce_fusion.2
  1704.4 172.4 %psum.46 = f32[]{:T(128)} all-reduce(f32[]{:T(128)} %get-tuple-element.8), channel_id=1, replica_groups=mesh['ref'=2,'lines'=8,'cells'=8] {'lines','cells'}, use_global_device_ids=true, to_apply=%region_20.0 | all-reduce | flops 1 | bytes 8 | tf_op jit(solution)/shard_map/psum | solution.py:76
  1878.1 174.2 %all_gather.15 = bf16[262144]{0:T(1024)(128)(2,1)S(1)} all-gather(bf16[4096]{0:T(1024)(128)(2,1)S(1)} %get-tuple-element.6), channel_id=1, replica_groups=mesh['ref'=2,'lines'=8,'cells'=8] {'lines','cells'}, dimensions={0}, use_global_device_ids=true | all-gather | bytes 532480 | tf_op jit(solution)/shard_map/all_gather | solution.py:53
  2052.3 1.3 gather_fusion.9
  2053.6 12.2 fusion.23
  2066.1 1.3 gather_fusion.10
  2067.5 8.1 fusion.21
  2075.5 3.3 scatter_custom_fusion.3
  2080.2 4.5 collective-permute-start.6
  2084.7 1.3 collective-permute-done.6
  2086.0 135.5 %gather_fusion.11 = f32[24576]{0:T(1024)S(1)} fusion(f32[6144]{0:T(1024)S(1)} %pad_maximum_fusion.3, s32[24576]{0:T(1024)S(1)} %broadcast_clamp_fusion), kind=kCustom, calls=%fused_computation.11 | custom fusion | bytes 294912 | tf_op jit(solution)/shard_map/gather | solution.py:72
  2222.9 1.3 multiply_reduce_fusion.1
  2224.9 174.5 %psum.47 = f32[]{:T(128)} all-reduce(f32[]{:T(128)S(6)} %add.118), channel_id=1, replica_groups=mesh['ref'=2,'lines'=8,'cells'=8] {'lines','cells'}, use_global_device_ids=true, to_apply=%region_26.0 | all-reduce | flops 1 | bytes 8 | tf_op jit(solution)/shard_map/psum | solution.py:90
  2400.7 1.3 multiply_subtract_fusion
  (66 shorter events, 10.9 us)
Async XLA Ops:
  7.2 350.8 %all-reduce.10.cloned.1.call-start = ((), (), s32[]{:S(2)}) async-start(), calls=%async_computation | async-start | bytes 2097152
  8.0 214.2 %collective-permute-start.1 = (f32[1024]{0:T(1024)S(1)}, f32[1024]{0:T(1024)S(1)}, u32[]{:S(2)}, u32[]{:S(2)}) collective-permute-start(f32[1024]{0:T(1024)S(1)} %get-tuple-element.28), channel_id=1, source_target_pairs={{1,0},{2,1},{3,2},{4,3},{5,4},{6,5},{7,6},{8,7},{9,8},{10,9},{11,1... | collective-permute-start | bytes 12296 | tf_op jit(solution)/shard_map/ppermute | solution.py:22
  9.3 212.9 %collective-permute-start = (f32[1024]{0:T(1024)S(1)}, f32[1024]{0:T(1024)S(1)}, u32[]{:S(2)}, u32[]{:S(2)}) collective-permute-start(f32[1024]{0:T(1024)S(1)} %get-tuple-element.27), channel_id=1, source_target_pairs={{0,1},{1,2},{2,3},{3,4},{4,5},{5,6},{6,7},{7,8},{8,9},{9,10},{10,1... | collective-permute-start | bytes 12296 | tf_op jit(solution)/shard_map/ppermute | solution.py:20
  195.5 12.3 copy-start.1
  195.5 12.3 copy-start.3
  195.5 12.3 copy-start.4
  207.8 13.1 copy-start.2
  207.8 13.2 copy-start.5
  220.8 605.5 %all-reduce.12.cloned.1.call-start = ((), (), s32[]{:S(2)}) async-start(), calls=%async_computation.1 | async-start | bytes 2097152
  222.3 135.7 %copy-start = (f32[4096]{0:T(1024)S(1)}, f32[4096]{0:T(1024)}, u32[]{:S(2)}) copy-start(f32[4096]{0:T(1024)} %param.15) | copy-start | bytes 49156
  358.7 5.9 collective-permute-start.3
  360.0 5.9 collective-permute-start.2
  703.0 822.2 %all-reduce.14.cloned.1.call-start = ((), (), s32[]{:S(2)}) async-start(), calls=%async_computation.2 | async-start | bytes 2097152
  1381.1 841.8 %all-reduce.16.cloned.1.call-start = ((), (), s32[]{:S(2)}) async-start(), calls=%async_computation.3 | async-start | bytes 2097152
  1381.2 5.9 collective-permute-start.5
  1382.5 5.9 collective-permute-start.4
  2078.9 5.9 collective-permute-start.7
  2080.2 5.9 collective-permute-start.6
Sparse Core Ops, SparseCore 0:
  220.9 123.0 all-reduce.9
  703.1 123.1 all-reduce.11
  1381.2 123.1 all-reduce.13
  2079.0 123.1 all-reduce.15
where the time goes:
time: 2410 us
  blocking collectives  1570 us (65%)
  local copies, waits for them, and re-layouts  554 us (23%)
  waiting for transfers between devices  127 us (5%)
  matrix products  82.1 us (3%)
  other arithmetic  26.2 us (1%)
  between operations  25.5 us (1%)
    all_gather x4, blocking collectives, forward(): gathered = lax.all_gather(vector, ('lines', 'cells'), axis=0, tiled=True)  702 us
    gather x8, local copies, waits for them, and re-layouts, smooth(): nearby = padded[local_index]  542 us
    psum x3, blocking collectives, squares(): return lax.psum(jnp.sum(residual * residual), ('lines', 'cells'))  520 us
    psum x2, blocking collectives, per_device(): lax.psum(jnp.sum(direction_half.astype(jnp.float32) * transposed) + beta_...  349 us
    unnamed x8, waiting for transfers between devices  123 us
    dot_general x4, matrix products, forward(): jnp.einsum('bij,bj->bi', sens, columns, preferred_element_type=jnp.float32)  48.9 us
  transfers between devices with their start and end apart: 12, of which 4 were waited for; matrix products, arithmetic and copies ran while one was open for 18% of the time, Pallas kernels for 0%

commit v1 on v0

v1 whole, which is shorter than its diff:
```python
import functools

import jax
import jax.numpy as jnp
from jax import lax
from jax.experimental import pallas as pl
from jax.experimental.pallas import tpu as pltpu
from jax.sharding import PartitionSpec as P

CG_STEPS = 3
beta_reg = 0.5

AXES = ("lines", "cells")
UNROLL = 4
GROUP_DEVS = 64
ROWS = 32
CELL_ROWS = 32
TABLE = GROUP_DEVS * CELL_ROWS
EXTRA = 16
F32 = jnp.float32
BF16 = jnp.bfloat16


def total(x):
    return jnp.sum(jnp.sum(x, axis=0, keepdims=True), axis=1, keepdims=True)


def smooth_from(win, nb_ref, small, offset):
    sub = lax.broadcasted_iota(jnp.int32, (8, 128), 0)
    pieces = []
    for g in range(CELL_ROWS // 8):
        acc = jnp.zeros((8, 128), F32)
        lanes = []
        deltas = []
        for k in range(6):
            index = nb_ref[k, pl.ds(8 * g, 8), :] - offset + 1024
            lanes.append(index & 127)
            deltas.append((index >> 7) - 8 * g - sub)
        for delta in range(17):
            source = win[pl.ds(8 * g + delta, 8), :]
            for k in range(6):
                picked = jnp.take_along_axis(source, lanes[k], axis=1, mode="promise_in_bounds")
                acc = acc + jnp.where(deltas[k] == delta, picked, 0.0)
        own = win[pl.ds(8 * g + 8, 8), :]
        pieces.append((small[pl.ds(8 * g, 8), :] + 6.0) * own - acc)
    return jnp.concatenate(pieces, axis=0)


def forward_rows(starts, order, cols, sens, tab, accs):
    def row(r, _):
        first = starts[r]
        count = (starts[r + 1] - first) // UNROLL

        def group(g, acc):
            for q in range(UNROLL):
                k = first + g * UNROLL + q
                acc = acc + sens[order[k]].astype(F32) * tab[pl.ds(cols[k], 1), :]
            return acc

        accs[r] = lax.fori_loop(0, count, group, jnp.zeros((128, 128), F32))
        return 0

    lax.fori_loop(0, ROWS, row, 0)


def reduce_rows(accs, pred):
    def rows(g, _):
        for q in range(4):
            r = g * 4 + q
            pred[pl.ds(r, 1), :] = jnp.sum(accs[r].T, axis=0, keepdims=True)
        return 0

    lax.fori_loop(0, ROWS // 4, rows, 0)


def backward_rows(starts, order, cols, sens, us, spread):
    spread[...] = jnp.zeros_like(spread)

    def row(r, _):
        first = starts[r]
        count = (starts[r + 1] - first) // UNROLL
        weights = jnp.broadcast_to(us[pl.ds(r, 1), :], (128, 128)).T

        def group(g, _):
            for q in range(UNROLL):
                k = first + g * UNROLL + q
                term = jnp.sum(sens[order[k]].astype(F32) * weights, axis=0, keepdims=True)
                spread[pl.ds(cols[k], 1), :] += term
            return 0

        lax.fori_loop(0, count, group, 0)
        return 0

    lax.fori_loop(0, ROWS, row, 0)


def write_payload(out, spread, scalar):
    if scalar is None:
        tail = jnp.zeros((EXTRA, 128), BF16)
    else:
        high = scalar.astype(BF16).astype(F32)
        middle = (scalar - high).astype(BF16).astype(F32)
        low = scalar - high - middle
        sub = lax.broadcasted_iota(jnp.int32, (EXTRA, 128), 0)
        lane = lax.broadcasted_iota(jnp.int32, (EXTRA, 128), 1)
        place = sub * 128 + lane
        tail = jnp.where(
            place == 0, high, jnp.where(place == 1, middle, jnp.where(place == 2, low, 0.0))
        ).astype(BF16)

    def owner(o, _):
        base = pl.multiple_of(o * CELL_ROWS, CELL_ROWS)
        out[o, pl.ds(0, CELL_ROWS), :] = spread[pl.ds(base, CELL_ROWS), :].astype(BF16)
        out[o, pl.ds(CELL_ROWS, EXTRA), :] = tail
        return 0

    lax.fori_loop(0, GROUP_DEVS, owner, 0)


def start_kernel(
    starts, order, cols, me, sens, recv, diff, observed, data_weight, nb, small,
    out, bent_out, tab, accs, pred, spread, win,
):
    def owner(o, _):
        base = pl.multiple_of(o * CELL_ROWS, CELL_ROWS)
        tab[pl.ds(base, CELL_ROWS), :] = recv[o, pl.ds(0, CELL_ROWS), :].astype(F32)
        return 0

    lax.fori_loop(0, GROUP_DEVS, owner, 0)
    tab[pl.ds(TABLE, 8), :] = jnp.zeros((8, 128), F32)
    mine = me[0]
    before = jnp.maximum(mine - 1, 0)
    after = jnp.minimum(mine + 1, GROUP_DEVS - 1)
    win[pl.ds(0, 8), :] = recv[before, pl.ds(CELL_ROWS, 16), :].astype(F32)[8:16]
    win[pl.ds(8, CELL_ROWS), :] = diff[...]
    win[pl.ds(8 + CELL_ROWS, 8), :] = recv[after, pl.ds(CELL_ROWS, 16), :].astype(F32)[0:8]
    bent_out[...] = smooth_from(win, nb, small, mine * (CELL_ROWS * 128))
    forward_rows(starts, order, cols, sens, tab, accs)
    reduce_rows(accs, pred)
    weight = data_weight[...]
    misfit = weight * weight * (pred[...] - observed[...])
    pred[...] = misfit.astype(BF16).astype(F32)
    backward_rows(starts, order, cols, sens, pred, spread)
    write_payload(out, spread, None)


def step_kernel(
    first_step,
    starts, order, cols, me, sens, recv, residual, direction, d_all_in, norm_in, data_weight, nb, small,
    out, bent_out, d_out, d_all_out, norm_out, tab, accs, pred, spread, win,
):
    def squares(o, acc):
        r = recv[o].astype(F32)
        return acc + r * r

    acc = lax.fori_loop(0, GROUP_DEVS, squares, jnp.zeros((CELL_ROWS, 128), F32))
    norm = total(acc)
    norm_out[...] = jnp.broadcast_to(norm, (8, 128))
    beta = None if first_step else norm / norm_in[0:1, 0:1]

    def owner(o, _):
        base = pl.multiple_of(o * CELL_ROWS, CELL_ROWS)
        d = recv[o].astype(F32)
        if not first_step:
            d = d + beta * d_all_in[pl.ds(base, CELL_ROWS), :]
        d_all_out[pl.ds(base, CELL_ROWS), :] = d
        tab[pl.ds(base, CELL_ROWS), :] = d.astype(BF16).astype(F32)
        return 0

    lax.fori_loop(0, GROUP_DEVS, owner, 0)
    tab[pl.ds(TABLE, 8), :] = jnp.zeros((8, 128), F32)
    d_own = residual[...]
    if not first_step:
        d_own = d_own + beta * direction[...]
    d_out[...] = d_own
    mine = me[0]
    base = mine * CELL_ROWS
    before = pl.multiple_of(jnp.maximum(base - 8, 0), 8)
    after = pl.multiple_of(jnp.minimum(base + CELL_ROWS, TABLE - 8), 8)
    win[pl.ds(0, 8), :] = d_all_out[pl.ds(before, 8), :]
    win[pl.ds(8, CELL_ROWS), :] = d_own
    win[pl.ds(8 + CELL_ROWS, 8), :] = d_all_out[pl.ds(after, 8), :]
    bent = smooth_from(win, nb, small, mine * (CELL_ROWS * 128))
    bent_out[...] = bent
    forward_rows(starts, order, cols, sens, tab, accs)
    reduce_rows(accs, pred)
    weight = data_weight[...]
    predicted = pred[...]
    weighted = (weight * weight * predicted).astype(BF16).astype(F32)
    curvature = total(predicted * weighted) + beta_reg * total(d_own * bent)
    pred[...] = weighted
    backward_rows(starts, order, cols, sens, pred, spread)
    write_payload(out, spread, curvature)


def gathered_sum(recv):
    def owner(o, acc):
        return acc + recv[o].astype(F32)

    return lax.fori_loop(0, GROUP_DEVS, owner, jnp.zeros((CELL_ROWS + EXTRA, 128), F32))


def broadcast_out(out, value):
    half = value.astype(BF16)

    def owner(o, _):
        out[o] = half
        return 0

    lax.fori_loop(0, GROUP_DEVS, owner, 0)


def right_side_kernel(recv, bent, r_out, out):
    sums = gathered_sum(recv)
    r = -(sums[:CELL_ROWS] + beta_reg * bent[...])
    r_out[...] = r
    broadcast_out(out, r)


def update_kernel(first_step, last_step, recv, bent, direction, residual, update, norm, u_out, r_out, *out):
    sums = gathered_sum(recv)
    curvature = total(sums[CELL_ROWS : CELL_ROWS + 8])
    alpha = norm[0:1, 0:1] / curvature
    d = direction[...]
    u_out[...] = alpha * d if first_step else update[...] + alpha * d
    r = residual[...] - alpha * (sums[:CELL_ROWS] + beta_reg * bent[...])
    r_out[...] = r
    if not last_step:
        broadcast_out(out[0], r)


VM = pl.BlockSpec(memory_space=pltpu.VMEM)
SM = pl.BlockSpec(memory_space=pltpu.SMEM)
PARAMS = pltpu.CompilerParams(vmem_limit_bytes=30 << 20)


def cells_shape():
    return jax.ShapeDtypeStruct((CELL_ROWS, 128), F32)


def scratch():
    return [
        pltpu.VMEM((TABLE + 8, 128), F32),
        pltpu.VMEM((ROWS, 128, 128), F32),
        pltpu.VMEM((ROWS, 128), F32),
        pltpu.VMEM((TABLE + 8, 128), F32),
        pltpu.VMEM((CELL_ROWS + 16, 128), F32),
    ]


def row_lists(block_rows, block_cols):
    blocks = block_rows.shape[0]
    longest = blocks + ROWS * (UNROLL - 1)
    ids = jnp.arange(blocks, dtype=jnp.int32)
    rows = jnp.arange(ROWS, dtype=jnp.int32)
    counts = jnp.sum((block_rows[None, :] == rows[:, None]).astype(jnp.int32), axis=1)
    padded = (counts + UNROLL - 1) // UNROLL * UNROLL
    starts = jnp.sum(
        jnp.where(rows[None, :] < jnp.arange(ROWS + 1, dtype=jnp.int32)[:, None], padded[None, :], 0), axis=1
    )
    earlier = (block_rows[None, :] == block_rows[:, None]) & (ids[None, :] < ids[:, None])
    lower = jnp.where(rows[None, :] < block_rows[:, None], padded[None, :], 0)
    place = jnp.sum(earlier.astype(jnp.int32), axis=1) + jnp.sum(lower, axis=1)
    hit = place[None, :] == jnp.arange(longest, dtype=jnp.int32)[:, None]
    order = jnp.sum(jnp.where(hit, ids[None, :], 0), axis=1)
    cols = TABLE + jnp.sum(jnp.where(hit, block_cols[None, :] - TABLE, 0), axis=1)
    return starts, order, cols


def per_device(
    sens, block_rows, block_cols, neighbours, observed, data_weight, smallness, model, reference_model
):
    starts, order, cols = row_lists(block_rows, block_cols)
    me = lax.axis_index(AXES).astype(jnp.int32).reshape(1)
    nb = neighbours.reshape(6, CELL_ROWS, 128)
    observed = observed.reshape(ROWS, 128)
    data_weight = data_weight.reshape(ROWS, 128)
    small = smallness.reshape(CELL_ROWS, 128)
    model = model.reshape(CELL_ROWS, 128)
    diff = model - reference_model.reshape(CELL_ROWS, 128)

    def exchange(x):
        return lax.all_to_all(x, AXES, 0, 0, tiled=True)

    payload = jnp.concatenate([model, diff[:8], diff[-8:]], axis=0).astype(BF16)
    recv = exchange(jnp.broadcast_to(payload[None], (GROUP_DEVS, CELL_ROWS + 16, 128)))
    sent = jax.ShapeDtypeStruct((GROUP_DEVS, CELL_ROWS + EXTRA, 128), BF16)
    gather = jax.ShapeDtypeStruct((GROUP_DEVS, CELL_ROWS, 128), BF16)
    sens = pltpu.with_memory_space_constraint(sens, pltpu.VMEM)
    out, bent = pl.pallas_call(
        start_kernel,
        out_shape=(sent, cells_shape()),
        in_specs=[SM] * 4 + [VM] * 7,
        out_specs=(VM, VM),
        scratch_shapes=scratch(),
        compiler_params=PARAMS,
        name="start",
    )(starts, order, cols, me, sens, recv, diff, observed, data_weight, nb, small)
    residual, out = pl.pallas_call(
        right_side_kernel,
        out_shape=(cells_shape(), gather),
        in_specs=[VM] * 2,
        out_specs=(VM, VM),
        compiler_params=PARAMS,
        name="right_side",
    )(exchange(out), bent)
    direction = residual
    update = residual
    d_all = jnp.zeros((8, 128), F32)
    norm = jnp.zeros((8, 128), F32)
    for step in range(CG_STEPS):
        first, last = step == 0, step == CG_STEPS - 1
        out, bent, direction, d_all, norm = pl.pallas_call(
            functools.partial(step_kernel, first),
            out_shape=(
                sent,
                cells_shape(),
                cells_shape(),
                jax.ShapeDtypeStruct((TABLE, 128), F32),
                jax.ShapeDtypeStruct((8, 128), F32),
            ),
            in_specs=[SM] * 4 + [VM] * 9,
            out_specs=(VM,) * 5,
            scratch_shapes=scratch(),
            compiler_params=PARAMS,
            name="step",
        )(starts, order, cols, me, sens, exchange(out), residual, direction, d_all, norm, data_weight, nb, small)
        results = pl.pallas_call(
            functools.partial(update_kernel, first, last),
            out_shape=(cells_shape(), cells_shape()) + (() if last else (gather,)),
            in_specs=[VM] * 6,
            out_specs=(VM,) * (2 if last else 3),
            compiler_params=PARAMS,
            name="update",
        )(exchange(out), bent, direction, residual, update, norm)
        update, residual = results[:2]
        if not last:
            out = results[2]
    return update.reshape(-1), residual.reshape(-1)


def solution(mesh):
    own = P(AXES)
    part = P(("ref",) + AXES)
    in_specs = (P(AXES, None, None), own, own, P(None, AXES), own, own, own, part, part)
    return jax.shard_map(
        per_device, mesh=mesh, in_specs=in_specs, out_specs=(part, part), check_vma=False
    )
```

time: 2410 us -> 261 us (0.11)
  blocking collectives: 1570 us -> 121 us
  local copies, waits for them, and re-layouts: 554 us -> 24.1 us
  waiting for transfers between devices: 127 us -> 15.1 us
  Pallas kernels: 0 us -> 85.8 us
  matrix products: 82.1 us -> 0 us
  between operations: 25.5 us -> 0.83 us
  other arithmetic: 26.2 us -> 1.8 us
    psum x5 -> x0, blocking collectives: 869 us -> none  [the longest x3 520 us: squares(): return lax.psum(jnp.sum(residual * residual), ('lines', 'cells'))]
    all_gather x4 -> x0, blocking collectives: 702 us -> none  [forward(): gathered = lax.all_gather(vector, ('lines', 'cells'), axis=0, tiled=True)]
    gather x16 -> x0, local copies, waits for them, and re-layouts: 553 us -> none  [the longest x8 542 us: smooth(): nearby = padded[local_index]]
    unnamed x8 -> x0, waiting for transfers between devices: 123 us -> none
    all_to_all x0 -> x7, blocking collectives: none -> 121 us  [exchange(): return lax.all_to_all(x, AXES, 0, 0, tiled=True)]
    pallas_call x0 -> x8, Pallas kernels: none -> 85.8 us  [the longest x3 63.5 us: per_device(): pl.pallas_call(functools.partial(step_kernel, first), out_shape=(sent, ce...]
    dot_general x12 -> x0, matrix products: 82.1 us -> none  [the longest x4 48.9 us: forward(): jnp.einsum('bij,bj->bi', sens, columns, preferred_element_type=jnp.float32)]
  transfers between devices with their start and end apart: 12 -> 1, of which waited for: 4 -> 1; matrix products, arithmetic and copies ran while one was open for 18% -> 0% of each run, Pallas kernels for 0% -> 0%
where the time goes in v1:
time: 261 us
  blocking collectives  121 us (46%)
  Pallas kernels  85.8 us (33%)
  local copies, waits for them, and re-layouts  24.1 us (9%)
  waiting for transfers between devices  15.1 us (6%)
  starting transfers between devices  11.5 us (4%)
    all_to_all x7, blocking collectives, exchange(): return lax.all_to_all(x, AXES, 0, 0, tiled=True)  121 us
    pallas_call x3, Pallas kernels, per_device(): pl.pallas_call(functools.partial(step_kernel, first), out_shape=(sent, ce...  63.5 us
    unnamed x21, local copies, waits for them, and re-layouts  23.1 us
    pallas_call x1, Pallas kernels, per_device(): pl.pallas_call(start_kernel, out_shape=(sent, cells_shape()), in_specs=[S...  18.9 us
    all_to_all x1, waiting for transfers between devices, exchange(): return lax.all_to_all(x, AXES, 0, 0, tiled=True)  15.1 us
    all_to_all x1, starting transfers between devices, exchange(): return lax.all_to_all(x, AXES, 0, 0, tiled=True)  11.5 us
  transfers between devices with their start and end apart: 1, of which 1 were waited for; matrix products, arithmetic and copies ran while one was open for 0% of the time, Pallas kernels for 0%

profile of v1, /device:TPU:0, one launch (start us, length us, event | category | flops | bytes accessed | tf_op | source)
XLA Modules:
  0.0 260.6 jit_solution(14507245090989988709)
XLA Ops:
  0.6 0.0 copy-start.8
  0.6 0.0 copy-start.7
  0.7 0.8 fusion.2
  1.5 0.0 copy-start.9
  1.5 0.0 copy-start.4
  1.5 0.0 copy-start.5
  1.5 0.0 copy-start.6
  1.5 1.0 broadcast_in_dim.71
  2.5 11.5 %all-to-all-start = ((bf16[64,48,128]{2,1,0:T(8,128)(2,1)}), bf16[64,48,128]{2,1,0:T(8,128)(2,1)S(1)}, u32[]{:S(2)}, u32[]{:S(2)}) async-start(bf16[64,48,128]{2,1,0:T(8,128)(2,1)} %broadcast_in_dim.71), calls=%async_computation | async-start | bytes 1572864 | tf_op jit(solution)/shard_map/all_to_all | solution.py:283
  14.0 0.0 copy-done.8
  14.0 0.1 convert_reduce_fusion.1
  14.1 0.3 convert_reduce_fusion
  14.4 0.1 select_reduce_fusion.2
  14.5 0.0 copy-done.7
  14.6 0.1 select_reduce_fusion.3.starts
  14.7 0.0 copy-done.9
  14.7 0.4 select_reduce_fusion
  15.1 15.1 %all-to-all-done.recv = bf16[64,48,128]{2,1,0:T(8,128)(2,1)S(1)} async-done(((bf16[64,48,128]{2,1,0:T(8,128)(2,1)}), bf16[64,48,128]{2,1,0:T(8,128)(2,1)S(1)}, u32[]{:S(2)}, u32[]{:S(2)}) %all-to-all-start) | async-done | bytes 786464 | tf_op jit(solution)/shard_map/all_to_all | solution.py:283
  30.2 0.0 copy-done.4
  30.2 0.0 copy-done.5
  30.2 0.0 copy-done.6
  30.2 0.0 copy-start
  30.2 5.8 %copy-done = bf16[512,128,128]{2,1,0:T(8,128)(2,1)S(1)} copy-done((bf16[512,128,128]{2,1,0:T(8,128)(2,1)S(1)}, bf16[512,128,128]{2,1,0:T(8,128)(2,1)}, u32[]{:S(2)}) %copy-start) | copy-done | bytes 16777240
  36.0 18.9 %start.1 = (bf16[64,48,128]{2,1,0:T(8,128)(2,1)S(1)}, f32[32,128]{1,0:T(8,128)S(1)}) custom-call(s32[33]{0:T(128)S(1)} %select_reduce_fusion.3.starts, s32[608]{0:T(1024)S(1)} %get-tuple-element.55.order, s32[608]{0:T(1024)S(1)} %broadcast_add_fusion.cols, s32[1]{0:T(128)} %bitcast.me, bf16[512,128,128]{2,1,0:T(8,128)(2,1)S(1)} %copy-done, ...), custom_call_target="tpu_custom_call" | custom-call | tf_op jit(solution)/shard_map/start/pallas_call | solution.py:290
  54.9 19.0 %all_to_all.40.recv = bf16[64,48,128]{2,1,0:T(8,128)(2,1)S(1)} all-to-all(bf16[64,48,128]{2,1,0:T(8,128)(2,1)S(1)} %get-tuple-element.28), channel_id=1, replica_groups=mesh['ref'=2,'lines'=8,'cells'=8] {'lines','cells'}, dimensions={0} | all-to-all | bytes 1572864 | tf_op jit(solution)/shard_map/all_to_all | solution.py:283
  74.0 0.7 right_side.1
  74.7 16.4 %all_to_all.41.recv = bf16[64,32,128]{2,1,0:T(8,128)(2,1)S(1)} all-to-all(bf16[64,32,128]{2,1,0:T(8,128)(2,1)S(1)} %get-tuple-element.30), channel_id=1, replica_groups=mesh['ref'=2,'lines'=8,'cells'=8] {'lines','cells'}, dimensions={0} | all-to-all | bytes 1048576 | tf_op jit(solution)/shard_map/all_to_all | solution.py:283
  91.1 0.0 copy-start.1
  91.1 5.8 %copy-done.1 = bf16[512,128,128]{2,1,0:T(8,128)(2,1)S(1)} copy-done((bf16[512,128,128]{2,1,0:T(8,128)(2,1)S(1)}, bf16[512,128,128]{2,1,0:T(8,128)(2,1)}, u32[]{:S(2)}) %copy-start.1) | copy-done | bytes 16777240
  96.8 19.4 %step.3 = (bf16[64,48,128]{2,1,0:T(8,128)(2,1)S(1)}, f32[32,128]{1,0:T(8,128)S(1)}, f32[32,128]{1,0:T(8,128)S(1)}, f32[2048,128]{1,0:T(8,128)S(1)}, f32[8,128]{1,0:T(8,128)S(1)}) custom-call(s32[33]{0:T(128)S(1)} %select_reduce_fusion.3.starts, s32[608]{0:T(1024)S(1)} %get-tuple-element.55.order, s32[608]{0:T(1024)S(1)} %broadcast_add_fusion.cols, ...), custom_call_target="tpu_custom_call" | custom-call | tf_op jit(solution)/shard_map/step/pallas_call | solution.py:313
  116.3 17.7 %all_to_all.42.recv = bf16[64,48,128]{2,1,0:T(8,128)(2,1)S(1)} all-to-all(bf16[64,48,128]{2,1,0:T(8,128)(2,1)S(1)} %get-tuple-element.32), channel_id=1, replica_groups=mesh['ref'=2,'lines'=8,'cells'=8] {'lines','cells'}, dimensions={0} | all-to-all | bytes 1572864 | tf_op jit(solution)/shard_map/all_to_all | solution.py:283
  134.0 0.8 update.3
  134.8 16.4 %all_to_all.43.recv = bf16[64,32,128]{2,1,0:T(8,128)(2,1)S(1)} all-to-all(bf16[64,32,128]{2,1,0:T(8,128)(2,1)S(1)} %get-tuple-element.36), channel_id=1, replica_groups=mesh['ref'=2,'lines'=8,'cells'=8] {'lines','cells'}, dimensions={0} | all-to-all | bytes 1048576 | tf_op jit(solution)/shard_map/all_to_all | solution.py:283
  151.2 0.0 copy-start.2
  151.2 5.8 %copy-done.2 = bf16[512,128,128]{2,1,0:T(8,128)(2,1)S(1)} copy-done((bf16[512,128,128]{2,1,0:T(8,128)(2,1)S(1)}, bf16[512,128,128]{2,1,0:T(8,128)(2,1)}, u32[]{:S(2)}) %copy-start.2) | copy-done | bytes 16777240
  157.0 21.5 %step.4 = (bf16[64,48,128]{2,1,0:T(8,128)(2,1)S(1)}, f32[32,128]{1,0:T(8,128)S(1)}, f32[32,128]{1,0:T(8,128)S(1)}, f32[2048,128]{1,0:T(8,128)S(1)}, f32[8,128]{1,0:T(8,128)S(1)}) custom-call(s32[33]{0:T(128)S(1)} %select_reduce_fusion.3.starts, s32[608]{0:T(1024)S(1)} %get-tuple-element.55.order, s32[608]{0:T(1024)S(1)} %broadcast_add_fusion.cols, ...), custom_call_target="tpu_custom_call" | custom-call | tf_op jit(solution)/shard_map/step/pallas_call | solution.py:313
  178.5 17.7 %all_to_all.44.recv = bf16[64,48,128]{2,1,0:T(8,128)(2,1)S(1)} all-to-all(bf16[64,48,128]{2,1,0:T(8,128)(2,1)S(1)} %get-tuple-element.39), channel_id=1, replica_groups=mesh['ref'=2,'lines'=8,'cells'=8] {'lines','cells'}, dimensions={0} | all-to-all | bytes 1572864 | tf_op jit(solution)/shard_map/all_to_all | solution.py:283
  196.3 0.8 update.4
  197.1 16.4 %all_to_all.45.recv = bf16[64,32,128]{2,1,0:T(8,128)(2,1)S(1)} all-to-all(bf16[64,32,128]{2,1,0:T(8,128)(2,1)S(1)} %get-tuple-element.44), channel_id=1, replica_groups=mesh['ref'=2,'lines'=8,'cells'=8] {'lines','cells'}, dimensions={0} | all-to-all | bytes 1048576 | tf_op jit(solution)/shard_map/all_to_all | solution.py:283
  213.5 0.0 copy-start.3
  213.5 5.8 %copy-done.3 = bf16[512,128,128]{2,1,0:T(8,128)(2,1)S(1)} copy-done((bf16[512,128,128]{2,1,0:T(8,128)(2,1)S(1)}, bf16[512,128,128]{2,1,0:T(8,128)(2,1)}, u32[]{:S(2)}) %copy-start.3) | copy-done | bytes 16777240
  219.3 22.5 %step.5 = (bf16[64,48,128]{2,1,0:T(8,128)(2,1)S(1)}, f32[32,128]{1,0:T(8,128)S(1)}, f32[32,128]{1,0:T(8,128)S(1)}, f32[2048,128]{1,0:T(8,128)}, f32[8,128]{1,0:T(8,128)S(1)}) custom-call(s32[33]{0:T(128)S(1)} %select_reduce_fusion.3.starts, s32[608]{0:T(1024)S(1)} %get-tuple-element.55.order, s32[608]{0:T(1024)S(1)} %broadcast_add_fusion.cols, s32[1]{0:T(128)} %bitcast.me, ...), custom_call_target="tpu_custom_call" | custom-call | tf_op jit(solution)/shard_map/step/pallas_call | solution.py:313
  241.8 17.7 %all_to_all.46.recv = bf16[64,48,128]{2,1,0:T(8,128)(2,1)S(1)} all-to-all(bf16[64,48,128]{2,1,0:T(8,128)(2,1)S(1)} %get-tuple-element.47), channel_id=1, replica_groups=mesh['ref'=2,'lines'=8,'cells'=8] {'lines','cells'}, dimensions={0} | all-to-all | bytes 1572864 | tf_op jit(solution)/shard_map/all_to_all | solution.py:283
  259.5 1.1 update.5
  (8 shorter events, 0.1 us)
Async XLA Ops:
  0.6 13.4 %copy-start.8 = (s32[512]{0:T(512)S(1)}, s32[512]{0:T(512)}, u32[]{:S(2)}) copy-start(s32[512]{0:T(512)} %param.10) | copy-start | bytes 6148
  0.6 13.9 %copy-start.7 = (s32[6,4096]{1,0:T(8,128)S(1)}, s32[6,4096]{1,0:T(8,128)}, u32[]{:S(2)}) copy-start(s32[6,4096]{1,0:T(8,128)} %param.12) | copy-start | bytes 294916
  1.5 13.2 %copy-start.9 = (s32[512]{0:T(512)S(1)}, s32[512]{0:T(512)}, u32[]{:S(2)}) copy-start(s32[512]{0:T(512)} %param.11) | copy-start | bytes 6148
  1.5 28.7 %copy-start.4 = (f32[4096]{0:T(1024)S(1)}, f32[4096]{0:T(1024)}, u32[]{:S(2)}) copy-start(f32[4096]{0:T(1024)} %param.14) | copy-start | bytes 49156
  1.5 28.7 %copy-start.5 = (f32[4096]{0:T(1024)S(1)}, f32[4096]{0:T(1024)}, u32[]{:S(2)}) copy-start(f32[4096]{0:T(1024)} %param.15) | copy-start | bytes 49156
  1.5 28.7 %copy-start.6 = (f32[4096]{0:T(1024)S(1)}, f32[4096]{0:T(1024)}, u32[]{:S(2)}) copy-start(f32[4096]{0:T(1024)} %param.13) | copy-start | bytes 49156
  2.5 27.7 %all-to-all-start = ((bf16[64,48,128]{2,1,0:T(8,128)(2,1)}), bf16[64,48,128]{2,1,0:T(8,128)(2,1)S(1)}, u32[]{:S(2)}, u32[]{:S(2)}) async-start(bf16[64,48,128]{2,1,0:T(8,128)(2,1)} %broadcast_in_dim.71), calls=%async_computation | async-start | bytes 1572864 | tf_op jit(solution)/shard_map/all_to_all | solution.py:283
  30.2 5.8 %copy-start = (bf16[512,128,128]{2,1,0:T(8,128)(2,1)S(1)}, bf16[512,128,128]{2,1,0:T(8,128)(2,1)}, u32[]{:S(2)}) copy-start(bf16[512,128,128]{2,1,0:T(8,128)(2,1)} %sens.7) | copy-start | bytes 50331652
  91.1 5.8 %copy-start.1 = (bf16[512,128,128]{2,1,0:T(8,128)(2,1)S(1)}, bf16[512,128,128]{2,1,0:T(8,128)(2,1)}, u32[]{:S(2)}) copy-start(bf16[512,128,128]{2,1,0:T(8,128)(2,1)} %sens.7) | copy-start | bytes 50331652
  151.2 5.8 %copy-start.2 = (bf16[512,128,128]{2,1,0:T(8,128)(2,1)S(1)}, bf16[512,128,128]{2,1,0:T(8,128)(2,1)}, u32[]{:S(2)}) copy-start(bf16[512,128,128]{2,1,0:T(8,128)(2,1)} %sens.7) | copy-start | bytes 50331652
  213.5 5.8 %copy-start.3 = (bf16[512,128,128]{2,1,0:T(8,128)(2,1)S(1)}, bf16[512,128,128]{2,1,0:T(8,128)(2,1)}, u32[]{:S(2)}) copy-start(bf16[512,128,128]{2,1,0:T(8,128)(2,1)} %sens.7) | copy-start | bytes 50331652

commit v2 on v1

v2 whole, which is shorter than its diff:
```python
import functools

import jax
import jax.numpy as jnp
from jax import lax
from jax.experimental import pallas as pl
from jax.experimental.pallas import tpu as pltpu
from jax.sharding import PartitionSpec as P

CG_STEPS = 3
beta_reg = 0.5

AXES = ("lines", "cells")
BLOCKS = 512
CHUNK = 128
BATCH = 16
GROUP_DEVS = 64
ROWS = 32
CELL_ROWS = 32
TABLE = GROUP_DEVS * CELL_ROWS
SLOTS = 16
EXTRA = 16
SENT_ROWS = SLOTS + EXTRA
F32 = jnp.float32
BF16 = jnp.bfloat16


def total(x):
    return jnp.sum(jnp.sum(x, axis=0, keepdims=True), axis=1, keepdims=True)


def smooth_from(win, nb_ref, small, offset):
    sub = lax.broadcasted_iota(jnp.int32, (8, 128), 0)
    pieces = []
    for g in range(CELL_ROWS // 8):
        acc = jnp.zeros((8, 128), F32)
        lanes = []
        deltas = []
        for k in range(6):
            index = nb_ref[k, pl.ds(8 * g, 8), :] - offset + 1024
            lanes.append(index & 127)
            deltas.append((index >> 7) - 8 * g - sub)
        for delta in range(17):
            source = win[pl.ds(8 * g + delta, 8), :]
            for k in range(6):
                picked = jnp.take_along_axis(source, lanes[k], axis=1, mode="promise_in_bounds")
                acc = acc + jnp.where(deltas[k] == delta, picked, 0.0)
        own = win[pl.ds(8 * g + 8, 8), :]
        pieces.append((small[pl.ds(8 * g, 8), :] + 6.0) * own - acc)
    return jnp.concatenate(pieces, axis=0)


def gather_columns(cols, tab, temp, lhs):
    def rows(g, _):
        for q in range(64):
            k = g * 64 + q
            temp[pl.ds(k, 1), :] = tab[pl.ds(cols[k], 1), :]
        return 0

    lax.fori_loop(0, BLOCKS // 64, rows, 0)
    lhs[...] = temp[...].astype(BF16)


def forward_blocks(sens, lhs, products, ready=None):
    def chunk(g, _):
        first = pl.multiple_of(g * CHUNK, CHUNK)
        if ready is not None:
            ready(g)
        for h in range(CHUNK // BATCH):
            base = first + h * BATCH
            right = sens[pl.ds(base, BATCH)].reshape(BATCH * 128, 128)
            out = lax.dot_general(
                lhs[pl.ds(base, BATCH), :], right, (((1,), (1,)), ((), ())), preferred_element_type=F32
            )
            for q in range(BATCH):
                products[pl.ds(base + q, 1), :] = out[q : q + 1, q * 128 : (q + 1) * 128]
        return 0

    lax.fori_loop(0, BLOCKS // CHUNK, chunk, 0)


def row_hot(rows):
    return (lax.broadcasted_iota(jnp.int32, (ROWS, BLOCKS), 0) == rows[...]).astype(BF16)


def sum_rows(hot, products):
    value = products[...]
    high = value.astype(BF16)
    rest = value - high.astype(F32)
    middle = rest.astype(BF16)
    low = (rest - middle.astype(F32)).astype(BF16)
    return (
        jnp.dot(hot, high, preferred_element_type=F32)
        + jnp.dot(hot, middle, preferred_element_type=F32)
        + jnp.dot(hot, low, preferred_element_type=F32)
    )


def backward_blocks(hot, weighted, slots, sens, lhs, spread):
    lhs[...] = lax.dot_general(
        hot, weighted, (((0,), (0,)), ((), ())), preferred_element_type=F32
    ).astype(BF16)
    spread[...] = jnp.zeros_like(spread)

    def chunk(g, _):
        first = pl.multiple_of(g * CHUNK, CHUNK)
        for h in range(CHUNK // BATCH):
            base = first + h * BATCH
            right = jnp.concatenate([sens[base + q] for q in range(BATCH)], axis=1)
            out = jnp.dot(lhs[pl.ds(base, BATCH), :], right, preferred_element_type=F32)
            for q in range(BATCH):
                spread[pl.ds(slots[base + q], 1), :] = out[q : q + 1, q * 128 : (q + 1) * 128]
        return 0

    lax.fori_loop(0, BLOCKS // CHUNK, chunk, 0)


def scalar_tile(scalar):
    high = scalar.astype(BF16).astype(F32)
    middle = (scalar - high).astype(BF16).astype(F32)
    low = scalar - high - middle
    sub = lax.broadcasted_iota(jnp.int32, (EXTRA, 128), 0)
    lane = lax.broadcasted_iota(jnp.int32, (EXTRA, 128), 1)
    place = sub * 128 + lane
    return jnp.where(
        place == 0, high, jnp.where(place == 1, middle, jnp.where(place == 2, low, 0.0))
    ).astype(BF16)


def write_payload(out, spread, tail_of):
    def owners(g, _):
        for q in range(8):
            o = g * 8 + q
            base = pl.multiple_of(o * SLOTS, SLOTS)
            out[o, pl.ds(0, SLOTS), :] = spread[pl.ds(base, SLOTS), :].astype(BF16)
            out[o, pl.ds(SLOTS, EXTRA), :] = tail_of(o)
        return 0

    lax.fori_loop(0, GROUP_DEVS // 8, owners, 0)


def start_kernel(
    cols, slots, me, sens_hbm, rows, recv, diff, observed, data_weight, nb, small, slot_hot,
    out, bent_out, temp, lhs, spread, win, tab, sens, sems,
):
    def part(g):
        span = pl.ds(pl.multiple_of(g * CHUNK, CHUNK), CHUNK)
        return pltpu.make_async_copy(sens_hbm.at[span], sens.at[span], sems.at[g])

    for g in range(BLOCKS // CHUNK):
        part(g).start()

    def owners(g, _):
        for q in range(8):
            o = g * 8 + q
            base = pl.multiple_of(o * CELL_ROWS, CELL_ROWS)
            tab[pl.ds(base, CELL_ROWS), :] = recv[o, pl.ds(0, CELL_ROWS), :].astype(F32)
        return 0

    lax.fori_loop(0, GROUP_DEVS // 8, owners, 0)
    mine = me[0]
    before = jnp.maximum(mine - 1, 0)
    after = jnp.minimum(mine + 1, GROUP_DEVS - 1)
    win[pl.ds(0, 8), :] = recv[before, pl.ds(CELL_ROWS, 16), :].astype(F32)[8:16]
    win[pl.ds(8, CELL_ROWS), :] = diff[...]
    win[pl.ds(8 + CELL_ROWS, 8), :] = recv[after, pl.ds(CELL_ROWS, 16), :].astype(F32)[0:8]
    bent_out[...] = smooth_from(win, nb, small, mine * (CELL_ROWS * 128))
    gather_columns(cols, tab, temp, lhs)
    forward_blocks(sens, lhs, temp, lambda g: part(g).wait())
    hot = row_hot(rows)
    weight = data_weight[...]
    misfit = weight * weight * (sum_rows(hot, temp) - observed[...])
    backward_blocks(hot, misfit.astype(BF16), slots, sens, lhs, spread)
    write_payload(out, spread, lambda o: slot_hot[o])


def step_kernel(
    first_step,
    cols, slots, me, sens, rows, recv, residual, direction, d_all_in, norm_in, data_weight, nb, small,
    out, bent_out, d_out, d_all_out, norm_out, temp, lhs, spread, win,
):
    def squares(g, acc):
        for q in range(8):
            r = recv[g * 8 + q].astype(F32)
            acc = acc + r * r
        return acc

    acc = lax.fori_loop(0, GROUP_DEVS // 8, squares, jnp.zeros((CELL_ROWS, 128), F32))
    norm = total(acc)
    norm_out[...] = jnp.broadcast_to(norm, (8, 128))
    beta = None if first_step else norm / norm_in[0:1, 0:1]

    def owners(g, _):
        for q in range(8):
            o = g * 8 + q
            base = pl.multiple_of(o * CELL_ROWS, CELL_ROWS)
            d = recv[o].astype(F32)
            if not first_step:
                d = d + beta * d_all_in[pl.ds(base, CELL_ROWS), :]
            d_all_out[pl.ds(base, CELL_ROWS), :] = d
        return 0

    lax.fori_loop(0, GROUP_DEVS // 8, owners, 0)
    d_own = residual[...]
    if not first_step:
        d_own = d_own + beta * direction[...]
    d_out[...] = d_own
    mine = me[0]
    base = mine * CELL_ROWS
    before = pl.multiple_of(jnp.maximum(base - 8, 0), 8)
    after = pl.multiple_of(jnp.minimum(base + CELL_ROWS, TABLE - 8), 8)
    win[pl.ds(0, 8), :] = d_all_out[pl.ds(before, 8), :]
    win[pl.ds(8, CELL_ROWS), :] = d_own
    win[pl.ds(8 + CELL_ROWS, 8), :] = d_all_out[pl.ds(after, 8), :]
    bent = smooth_from(win, nb, small, mine * (CELL_ROWS * 128))
    bent_out[...] = bent
    gather_columns(cols, d_all_out, temp, lhs)
    forward_blocks(sens, lhs, temp)
    hot = row_hot(rows)
    weight = data_weight[...]
    predicted = sum_rows(hot, temp)
    weighted = (weight * weight * predicted).astype(BF16)
    curvature = total(predicted * weighted.astype(F32)) + beta_reg * total(d_own * bent)
    backward_blocks(hot, weighted, slots, sens, lhs, spread)
    tail = scalar_tile(curvature)
    write_payload(out, spread, lambda o: tail)


def gathered_sum(recv, pick):
    values = recv[:, 0:SLOTS, :].reshape(GROUP_DEVS * SLOTS, 128)
    return jnp.dot(pick, values, preferred_element_type=F32)


def broadcast_out(out, value):
    half = value.astype(BF16)

    def owners(g, _):
        for q in range(8):
            out[g * 8 + q] = half
        return 0

    lax.fori_loop(0, GROUP_DEVS // 8, owners, 0)


def right_side_kernel(recv, bent, r_out, out, pick_out):
    hot = recv[:, SLOTS : SLOTS + EXTRA, :].reshape(GROUP_DEVS * SLOTS, 128)
    pick = hot.astype(F32).T[:CELL_ROWS].astype(BF16)
    pick_out[...] = pick
    r = -(gathered_sum(recv, pick) + beta_reg * bent[...])
    r_out[...] = r
    broadcast_out(out, r)


def update_kernel(first_step, last_step, recv, pick, bent, direction, residual, update, norm, u_out, r_out, *out):
    sums = gathered_sum(recv, pick[...])

    def tails(g, acc):
        for q in range(8):
            acc = acc + recv[g * 8 + q, pl.ds(SLOTS, EXTRA), :].astype(F32)
        return acc

    curvature = total(lax.fori_loop(0, GROUP_DEVS // 8, tails, jnp.zeros((EXTRA, 128), F32)))
    alpha = norm[0:1, 0:1] / curvature
    d = direction[...]
    u_out[...] = alpha * d if first_step else update[...] + alpha * d
    r = residual[...] - alpha * (sums + beta_reg * bent[...])
    r_out[...] = r
    if not last_step:
        broadcast_out(out[0], r)


VM = pl.BlockSpec(memory_space=pltpu.VMEM)
SM = pl.BlockSpec(memory_space=pltpu.SMEM)
PARAMS = pltpu.CompilerParams(vmem_limit_bytes=12 << 20)


def cells_shape():
    return jax.ShapeDtypeStruct((CELL_ROWS, 128), F32)


def scratch():
    return [
        pltpu.VMEM((BLOCKS, 128), F32),
        pltpu.VMEM((BLOCKS, 128), BF16),
        pltpu.VMEM((GROUP_DEVS * SLOTS, 128), F32),
        pltpu.VMEM((CELL_ROWS + 16, 128), F32),
    ]


def slot_lists(block_cols):
    ids = jnp.arange(BLOCKS, dtype=jnp.int32)
    owners = block_cols // CELL_ROWS
    shared = (owners[None, :] == owners[:, None]) & (ids[None, :] < ids[:, None])
    slots = owners * SLOTS + jnp.sum(shared.astype(jnp.int32), axis=1)
    taken = slots[None, :] == jnp.arange(GROUP_DEVS * SLOTS, dtype=jnp.int32)[:, None]
    cell = jnp.sum(jnp.where(taken, (block_cols % CELL_ROWS)[None, :] + 1, 0), axis=1) - 1
    hot = (cell[:, None] == jnp.arange(128, dtype=jnp.int32)[None, :]).astype(BF16)
    return slots, hot.reshape(GROUP_DEVS, SLOTS, 128)


def per_device(
    sens, block_rows, block_cols, neighbours, observed, data_weight, smallness, model, reference_model
):
    cols = block_cols
    slots, slot_hot = slot_lists(block_cols)
    rows = block_rows.reshape(1, BLOCKS)
    me = lax.axis_index(AXES).astype(jnp.int32).reshape(1)
    nb = neighbours.reshape(6, CELL_ROWS, 128)
    observed = observed.reshape(ROWS, 128)
    data_weight = data_weight.reshape(ROWS, 128)
    small = smallness.reshape(CELL_ROWS, 128)
    model = model.reshape(CELL_ROWS, 128)
    diff = model - reference_model.reshape(CELL_ROWS, 128)

    def exchange(x):
        return lax.all_to_all(x, AXES, 0, 0, tiled=True)

    payload = jnp.concatenate([model, diff[:8], diff[-8:]], axis=0).astype(BF16)
    recv = exchange(jnp.broadcast_to(payload[None], (GROUP_DEVS, CELL_ROWS + 16, 128)))
    sent = jax.ShapeDtypeStruct((GROUP_DEVS, SENT_ROWS, 128), BF16)
    gather = jax.ShapeDtypeStruct((GROUP_DEVS, CELL_ROWS, 128), BF16)
    out, bent = pl.pallas_call(
        start_kernel,
        out_shape=(sent, cells_shape()),
        in_specs=[SM] * 3 + [pl.BlockSpec(memory_space=pltpu.HBM)] + [VM] * 8,
        out_specs=(VM, VM),
        scratch_shapes=scratch()
        + [
            pltpu.VMEM((TABLE, 128), F32),
            pltpu.VMEM((BLOCKS, 128, 128), BF16),
            pltpu.SemaphoreType.DMA((BLOCKS // CHUNK,)),
        ],
        compiler_params=pltpu.CompilerParams(vmem_limit_bytes=26 << 20),
        name="start",
    )(cols, slots, me, pltpu.with_memory_space_constraint(sens, pltpu.HBM), rows, recv, diff, observed, data_weight, nb, small, slot_hot)
    sens = pltpu.with_memory_space_constraint(sens, pltpu.VMEM)
    residual, out, pick = pl.pallas_call(
        right_side_kernel,
        out_shape=(cells_shape(), gather, jax.ShapeDtypeStruct((CELL_ROWS, GROUP_DEVS * SLOTS), BF16)),
        in_specs=[VM] * 2,
        out_specs=(VM,) * 3,
        compiler_params=PARAMS,
        name="right_side",
    )(exchange(out), bent)
    direction = residual
    update = residual
    d_all = jnp.zeros((8, 128), F32)
    norm = jnp.zeros((8, 128), F32)
    for step in range(CG_STEPS):
        first, last = step == 0, step == CG_STEPS - 1
        out, bent, direction, d_all, norm = pl.pallas_call(
            functools.partial(step_kernel, first),
            out_shape=(
                sent,
                cells_shape(),
                cells_shape(),
                jax.ShapeDtypeStruct((TABLE, 128), F32),
                jax.ShapeDtypeStruct((8, 128), F32),
            ),
            in_specs=[SM] * 3 + [VM] * 10,
            out_specs=(VM,) * 5,
            scratch_shapes=scratch(),
            compiler_params=PARAMS,
            name="step",
        )(cols, slots, me, sens, rows, exchange(out), residual, direction, d_all, norm, data_weight, nb, small)
        results = pl.pallas_call(
            functools.partial(update_kernel, first, last),
            out_shape=(cells_shape(), cells_shape()) + (() if last else (gather,)),
            in_specs=[VM] * 7,
            out_specs=(VM,) * (2 if last else 3),
            compiler_params=PARAMS,
            name="update",
        )(exchange(out), pick, bent, direction, residual, update, norm)
        update, residual = results[:2]
        if not last:
            out = results[2]
    return update.reshape(-1), residual.reshape(-1)


def solution(mesh):
    own = P(AXES)
    part = P(("ref",) + AXES)
    in_specs = (P(AXES, None, None), own, own, P(None, AXES), own, own, own, part, part)
    return jax.shard_map(
        per_device, mesh=mesh, in_specs=in_specs, out_specs=(part, part), check_vma=False
    )
```

time: 261 us -> 193 us (0.74)
  Pallas kernels: 85.8 us -> 46.4 us
  local copies, waits for them, and re-layouts: 24.1 us -> 1.15 us
  blocking collectives: 121 us -> 115 us
    pallas_call x3, Pallas kernels: 63.5 us -> 33 us  [per_device(): pl.pallas_call(functools.partial(step_kernel, first), out_shape=(sent, ce...]
    unnamed x21 -> x15, local copies, waits for them, and re-layouts: 23.1 us -> 0.05 us
    pallas_call x1, Pallas kernels: 18.9 us -> 11.6 us  [per_device(): pl.pallas_call(start_kernel, out_shape=(sent, cells_shape()), in_specs=[S...]
    all_to_all x7, blocking collectives: 121 us -> 115 us  [exchange(): return lax.all_to_all(x, AXES, 0, 0, tiled=True)]
where the time goes in v2:
time: 193 us; the launch traced here: 192 us
  blocking collectives  115 us (60%)
  Pallas kernels  46.4 us (24%)
  waiting for transfers between devices  15.3 us (8%)
  starting transfers between devices  11.5 us (6%)
    all_to_all x7, blocking collectives, exchange(): return lax.all_to_all(x, AXES, 0, 0, tiled=True)  115 us
    pallas_call x3, Pallas kernels, per_device(): pl.pallas_call(functools.partial(step_kernel, first), out_shape=(sent, ce...  33 us
    all_to_all x1, waiting for transfers between devices, exchange(): return lax.all_to_all(x, AXES, 0, 0, tiled=True)  15.3 us
    pallas_call x1, Pallas kernels, per_device(): pl.pallas_call(start_kernel, out_shape=(sent, cells_shape()), in_specs=[S...  11.6 us
    all_to_all x1, starting transfers between devices, exchange(): return lax.all_to_all(x, AXES, 0, 0, tiled=True)  11.5 us
  transfers between devices with their start and end apart: 1, of which 1 were waited for; matrix products, arithmetic and copies ran while one was open for 0% of the time, Pallas kernels for 0%

profile of v2, /device:TPU:0, one launch (start us, length us, event | category | flops | bytes accessed | tf_op | source)
XLA Modules:
  0.0 192.3 jit_solution(1152881074365324442)
XLA Ops:
  0.6 0.0 copy-start.3
  0.6 0.0 copy-start.6
  0.7 0.0 copy-start.2
  0.7 0.0 copy-start.1
  0.7 0.0 copy-start.5
  0.7 0.0 copy-start.4
  0.7 0.8 fusion.4
  1.5 1.0 broadcast_in_dim.10
  2.6 11.5 %all-to-all-start = ((bf16[64,48,128]{2,1,0:T(8,128)(2,1)}), bf16[64,48,128]{2,1,0:T(8,128)(2,1)S(1)}, u32[]{:S(2)}, u32[]{:S(2)}) async-start(bf16[64,48,128]{2,1,0:T(8,128)(2,1)} %broadcast_in_dim.10), calls=%async_computation | async-start | bytes 1572864 | tf_op jit(solution)/shard_map/all_to_all | solution.py:316
  14.1 0.0 copy-done.3
  14.1 0.2 convert_reduce_fusion
  14.4 0.3 select_reduce_fusion
  14.7 0.1 sub.18
  14.7 0.0 copy-done.6
  14.8 0.2 fusion.1.slot_hot
  15.0 15.3 %all-to-all-done.recv = bf16[64,48,128]{2,1,0:T(8,128)(2,1)S(1)} async-done(((bf16[64,48,128]{2,1,0:T(8,128)(2,1)}), bf16[64,48,128]{2,1,0:T(8,128)(2,1)S(1)}, u32[]{:S(2)}, u32[]{:S(2)}) %all-to-all-start) | async-done | bytes 786464 | tf_op jit(solution)/shard_map/all_to_all | solution.py:316
  30.2 0.0 copy-done.2
  30.2 0.0 copy-done.1
  30.2 0.0 copy-done.5
  30.3 0.0 copy-done.4
  30.3 0.0 copy-start
  30.3 11.6 %start.1 = (bf16[64,32,128]{2,1,0:T(8,128)(2,1)S(1)}, f32[32,128]{1,0:T(8,128)S(1)}) custom-call(s32[512]{0:T(512)S(1)} %copy-done.3, s32[512]{0:T(512)S(1)} %multiply_add_fusion.slots, s32[1]{0:T(128)} %bitcast.me, bf16[512,128,128]{2,1,0:T(8,128)(2,1)} %sens.5, s32[1,512]{1,0:T(1,128)S(1)} %bitcast.28, bf16[64,48,128]{2,1,0:T(8,128)(2,1)S(1)} %all-to-all-done.recv, ...), custom_call_target="tpu_custom_call" | custom-call | tf_op jit(solution)/shard_map/start/pallas_call | solution.py:322
  41.9 16.5 %all_to_all.40.recv = bf16[64,32,128]{2,1,0:T(8,128)(2,1)S(1)} all-to-all(bf16[64,32,128]{2,1,0:T(8,128)(2,1)S(1)} %get-tuple-element.29), channel_id=1, replica_groups=mesh['ref'=2,'lines'=8,'cells'=8] {'lines','cells'}, dimensions={0} | all-to-all | bytes 1048576 | tf_op jit(solution)/shard_map/all_to_all | solution.py:316
  58.4 0.3 right_side.1
  58.7 16.5 %all_to_all.41.recv = bf16[64,32,128]{2,1,0:T(8,128)(2,1)S(1)} all-to-all(bf16[64,32,128]{2,1,0:T(8,128)(2,1)S(1)} %get-tuple-element.31), channel_id=1, replica_groups=mesh['ref'=2,'lines'=8,'cells'=8] {'lines','cells'}, dimensions={0} | all-to-all | bytes 1048576 | tf_op jit(solution)/shard_map/all_to_all | solution.py:316
  75.2 0.0 copy-done
  75.2 10.5 %step.3 = (bf16[64,32,128]{2,1,0:T(8,128)(2,1)S(1)}, f32[32,128]{1,0:T(8,128)S(1)}, f32[32,128]{1,0:T(8,128)S(1)}, f32[2048,128]{1,0:T(8,128)S(1)}, f32[8,128]{1,0:T(8,128)S(1)}) custom-call(s32[512]{0:T(512)S(1)} %copy-done.3, s32[512]{0:T(512)S(1)} %multiply_add_fusion.slots, s32[1]{0:T(128)} %bitcast.me, bf16[512,128,128]{2,1,0:T(8,128)(2,1)S(1)} %copy-done, ...), custom_call_target="tpu_custom_call" | custom-call | tf_op jit(solution)/shard_map/step/pallas_call | solution.py:351
  85.7 16.5 %all_to_all.42.recv = bf16[64,32,128]{2,1,0:T(8,128)(2,1)S(1)} all-to-all(bf16[64,32,128]{2,1,0:T(8,128)(2,1)S(1)} %get-tuple-element.33), channel_id=1, replica_groups=mesh['ref'=2,'lines'=8,'cells'=8] {'lines','cells'}, dimensions={0} | all-to-all | bytes 1048576 | tf_op jit(solution)/shard_map/all_to_all | solution.py:316
  102.2 0.3 update.3
  102.5 16.5 %all_to_all.43.recv = bf16[64,32,128]{2,1,0:T(8,128)(2,1)S(1)} all-to-all(bf16[64,32,128]{2,1,0:T(8,128)(2,1)S(1)} %get-tuple-element.38), channel_id=1, replica_groups=mesh['ref'=2,'lines'=8,'cells'=8] {'lines','cells'}, dimensions={0} | all-to-all | bytes 1048576 | tf_op jit(solution)/shard_map/all_to_all | solution.py:316
  119.0 10.8 %step.4 = (bf16[64,32,128]{2,1,0:T(8,128)(2,1)S(1)}, f32[32,128]{1,0:T(8,128)S(1)}, f32[32,128]{1,0:T(8,128)S(1)}, f32[2048,128]{1,0:T(8,128)S(1)}, f32[8,128]{1,0:T(8,128)S(1)}) custom-call(s32[512]{0:T(512)S(1)} %copy-done.3, s32[512]{0:T(512)S(1)} %multiply_add_fusion.slots, s32[1]{0:T(128)} %bitcast.me, bf16[512,128,128]{2,1,0:T(8,128)(2,1)S(1)} %copy-done, ...), custom_call_target="tpu_custom_call" | custom-call | tf_op jit(solution)/shard_map/step/pallas_call | solution.py:351
  129.8 16.5 %all_to_all.44.recv = bf16[64,32,128]{2,1,0:T(8,128)(2,1)S(1)} all-to-all(bf16[64,32,128]{2,1,0:T(8,128)(2,1)S(1)} %get-tuple-element.41), channel_id=1, replica_groups=mesh['ref'=2,'lines'=8,'cells'=8] {'lines','cells'}, dimensions={0} | all-to-all | bytes 1048576 | tf_op jit(solution)/shard_map/all_to_all | solution.py:316
  146.3 0.3 update.4
  146.6 16.5 %all_to_all.45.recv = bf16[64,32,128]{2,1,0:T(8,128)(2,1)S(1)} all-to-all(bf16[64,32,128]{2,1,0:T(8,128)(2,1)S(1)} %get-tuple-element.46), channel_id=1, replica_groups=mesh['ref'=2,'lines'=8,'cells'=8] {'lines','cells'}, dimensions={0} | all-to-all | bytes 1048576 | tf_op jit(solution)/shard_map/all_to_all | solution.py:316
  163.1 11.8 %step.5 = (bf16[64,32,128]{2,1,0:T(8,128)(2,1)S(1)}, f32[32,128]{1,0:T(8,128)S(1)}, f32[32,128]{1,0:T(8,128)S(1)}, f32[2048,128]{1,0:T(8,128)}, f32[8,128]{1,0:T(8,128)S(1)}) custom-call(s32[512]{0:T(512)S(1)} %copy-done.3, s32[512]{0:T(512)S(1)} %multiply_add_fusion.slots, s32[1]{0:T(128)} %bitcast.me, bf16[512,128,128]{2,1,0:T(8,128)(2,1)S(1)} %copy-done, ...), custom_call_target="tpu_custom_call" | custom-call | tf_op jit(solution)/shard_map/step/pallas_call | solution.py:351
  174.9 16.5 %all_to_all.46.recv = bf16[64,32,128]{2,1,0:T(8,128)(2,1)S(1)} all-to-all(bf16[64,32,128]{2,1,0:T(8,128)(2,1)S(1)} %get-tuple-element.49), channel_id=1, replica_groups=mesh['ref'=2,'lines'=8,'cells'=8] {'lines','cells'}, dimensions={0} | all-to-all | bytes 1048576 | tf_op jit(solution)/shard_map/all_to_all | solution.py:316
  191.3 0.9 update.5
  (7 shorter events, 0.1 us)
Async XLA Ops:
  0.6 13.4 %copy-start.3 = (s32[512]{0:T(512)S(1)}, s32[512]{0:T(512)}, u32[]{:S(2)}) copy-start(s32[512]{0:T(512)} %cols.7) | copy-start | bytes 6148
  0.6 14.1 %copy-start.6 = (s32[6,4096]{1,0:T(8,128)S(1)}, s32[6,4096]{1,0:T(8,128)}, u32[]{:S(2)}) copy-start(s32[6,4096]{1,0:T(8,128)} %param.12) | copy-start | bytes 294916
  0.7 29.6 %copy-start.2 = (f32[4096]{0:T(1024)S(1)}, f32[4096]{0:T(1024)}, u32[]{:S(2)}) copy-start(f32[4096]{0:T(1024)} %param.15) | copy-start | bytes 49156
  0.7 29.6 %copy-start.1 = (f32[4096]{0:T(1024)S(1)}, f32[4096]{0:T(1024)}, u32[]{:S(2)}) copy-start(f32[4096]{0:T(1024)} %param.14) | copy-start | bytes 49156
  0.7 29.6 %copy-start.5 = (f32[4096]{0:T(1024)S(1)}, f32[4096]{0:T(1024)}, u32[]{:S(2)}) copy-start(f32[4096]{0:T(1024)} %param.13) | copy-start | bytes 49156
  0.7 29.6 %copy-start.4 = (s32[512]{0:T(512)S(1)}, s32[512]{0:T(512)}, u32[]{:S(2)}) copy-start(s32[512]{0:T(512)} %param.10) | copy-start | bytes 6148
  2.6 27.7 %all-to-all-start = ((bf16[64,48,128]{2,1,0:T(8,128)(2,1)}), bf16[64,48,128]{2,1,0:T(8,128)(2,1)S(1)}, u32[]{:S(2)}, u32[]{:S(2)}) async-start(bf16[64,48,128]{2,1,0:T(8,128)(2,1)} %broadcast_in_dim.10), calls=%async_computation | async-start | bytes 1572864 | tf_op jit(solution)/shard_map/all_to_all | solution.py:316
  30.3 44.9 %copy-start = (bf16[512,128,128]{2,1,0:T(8,128)(2,1)S(1)}, bf16[512,128,128]{2,1,0:T(8,128)(2,1)}, u32[]{:S(2)}) copy-start(bf16[512,128,128]{2,1,0:T(8,128)(2,1)} %sens.5) | copy-start | bytes 50331652

commit v3 on v2

--- a/solution.py
+++ b/solution.py
@@ -29,49 +29,44 @@
     return jnp.sum(jnp.sum(x, axis=0, keepdims=True), axis=1, keepdims=True)
 
 
-def smooth_from(win, nb_ref, small, offset):
+def smooth_group(g, win, nb_ref, small, offset, out):
+    first = pl.multiple_of(g * 8, 8)
     sub = lax.broadcasted_iota(jnp.int32, (8, 128), 0)
-    pieces = []
-    for g in range(CELL_ROWS // 8):
-        acc = jnp.zeros((8, 128), F32)
-        lanes = []
-        deltas = []
+    acc = jnp.zeros((8, 128), F32)
+    lanes = []
+    deltas = []
+    for k in range(6):
+        index = nb_ref[k, pl.ds(first, 8), :] - offset + 1024
+        lanes.append(index & 127)
+        deltas.append((index >> 7) - first - sub)
+    for delta in range(17):
+        source = win[pl.ds(first + delta, 8), :]
         for k in range(6):
-            index = nb_ref[k, pl.ds(8 * g, 8), :] - offset + 1024
-            lanes.append(index & 127)
-            deltas.append((index >> 7) - 8 * g - sub)
-        for delta in range(17):
-            source = win[pl.ds(8 * g + delta, 8), :]
-            for k in range(6):
-                picked = jnp.take_along_axis(source, lanes[k], axis=1, mode="promise_in_bounds")
-                acc = acc + jnp.where(deltas[k] == delta, picked, 0.0)
-        own = win[pl.ds(8 * g + 8, 8), :]
-        pieces.append((small[pl.ds(8 * g, 8), :] + 6.0) * own - acc)
-    return jnp.concatenate(pieces, axis=0)
-
-
-def gather_columns(cols, tab, temp, lhs):
-    def rows(g, _):
-        for q in range(64):
-            k = g * 64 + q
-            temp[pl.ds(k, 1), :] = tab[pl.ds(cols[k], 1), :]
-        return 0
-
-    lax.fori_loop(0, BLOCKS // 64, rows, 0)
-    lhs[...] = temp[...].astype(BF16)
-
-
-def forward_blocks(sens, lhs, products, ready=None):
+            picked = jnp.take_along_axis(source, lanes[k], axis=1, mode="promise_in_bounds")
+            acc = acc + jnp.where(deltas[k] == delta, picked, 0.0)
+    own = win[pl.ds(first + 8, 8), :]
+    out[pl.ds(first, 8), :] = (small[pl.ds(first, 8), :] + 6.0) * own - acc
+
+
+def forward_blocks(flipped, cols, tab, temp, products, beside, flip=None):
     def chunk(g, _):
         first = pl.multiple_of(g * CHUNK, CHUNK)
-        if ready is not None:
-            ready(g)
+        if flip is not None:
+            sens, wait = flip
+            wait(g)
+        beside(g)
         for h in range(CHUNK // BATCH):
             base = first + h * BATCH
-            right = sens[pl.ds(base, BATCH)].reshape(BATCH * 128, 128)
-            out = lax.dot_general(
-                lhs[pl.ds(base, BATCH), :], right, (((1,), (1,)), ((), ())), preferred_element_type=F32
-            )
+            for q in range(BATCH):
+                temp[pl.ds(base + q, 1), :] = tab[pl.ds(cols[base + q], 1), :]
+            left = temp[pl.ds(base, BATCH), :].astype(BF16)
+            if flip is not None:
+                blocks = [sens[base + q].T for q in range(BATCH)]
+                for q in range(BATCH):
+                    flipped[base + q] = blocks[q]
+            else:
+                blocks = [flipped[base + q] for q in range(BATCH)]
+            out = jnp.dot(left, jnp.concatenate(blocks, axis=1), preferred_element_type=F32)
             for q in range(BATCH):
                 products[pl.ds(base + q, 1), :] = out[q : q + 1, q * 128 : (q + 1) * 128]
         return 0
@@ -139,9 +134,22 @@
     lax.fori_loop(0, GROUP_DEVS // 8, owners, 0)
 
 
+def model_kernel(model, reference_model, diff_out, out):
+    diff = model[...] - reference_model[...]
+    diff_out[...] = diff
+    half = jnp.concatenate([model[...], diff[:8], diff[-8:]], axis=0).astype(BF16)
+
+    def owners(g, _):
+        for q in range(8):
+            out[g * 8 + q] = half
+        return 0
+
+    lax.fori_loop(0, GROUP_DEVS // 8, owners, 0)
+
+
 def start_kernel(
     cols, slots, me, sens_hbm, rows, recv, diff, observed, data_weight, nb, small, slot_hot,
-    out, bent_out, temp, lhs, spread, win, tab, sens, sems,
+    out, bent_out, sens, flipped, temp, products, lhs, spread, win, tab, sems,
 ):
     def part(g):
         span = pl.ds(pl.multiple_of(g * CHUNK, CHUNK), CHUNK)
@@ -164,20 +172,21 @@
     win[pl.ds(0, 8), :] = recv[before, pl.ds(CELL_ROWS, 16), :].astype(F32)[8:16]
     win[pl.ds(8, CELL_ROWS), :] = diff[...]
     win[pl.ds(8 + CELL_ROWS, 8), :] = recv[after, pl.ds(CELL_ROWS, 16), :].astype(F32)[0:8]
-    bent_out[...] = smooth_from(win, nb, small, mine * (CELL_ROWS * 128))
-    gather_columns(cols, tab, temp, lhs)
-    forward_blocks(sens, lhs, temp, lambda g: part(g).wait())
+    beside = functools.partial(
+        smooth_group, win=win, nb_ref=nb, small=small, offset=mine * (CELL_ROWS * 128), out=bent_out
+    )
+    forward_blocks(flipped, cols, tab, temp, products, beside, (sens, lambda g: part(g).wait()))
     hot = row_hot(rows)
     weight = data_weight[...]
-    misfit = weight * weight * (sum_rows(hot, temp) - observed[...])
+    misfit = weight * weight * (sum_rows(hot, products) - observed[...])
     backward_blocks(hot, misfit.astype(BF16), slots, sens, lhs, spread)
     write_payload(out, spread, lambda o: slot_hot[o])
 
 
 def step_kernel(
     first_step,
-    cols, slots, me, sens, rows, recv, residual, direction, d_all_in, norm_in, data_weight, nb, small,
-    out, bent_out, d_out, d_all_out, norm_out, temp, lhs, spread, win,
+    cols, slots, me, sens, flipped, rows, recv, residual, direction, d_all_in, norm_in, data_weight, nb, small,
+    out, bent_out, d_out, d_all_out, norm_out, temp, products, lhs, spread, win,
 ):
     def squares(g, acc):
         for q in range(8):
@@ -212,15 +221,15 @@
     win[pl.ds(0, 8), :] = d_all_out[pl.ds(before, 8), :]
     win[pl.ds(8, CELL_ROWS), :] = d_own
     win[pl.ds(8 + CELL_ROWS, 8), :] = d_all_out[pl.ds(after, 8), :]
-    bent = smooth_from(win, nb, small, mine * (CELL_ROWS * 128))
-    bent_out[...] = bent
-    gather_columns(cols, d_all_out, temp, lhs)
-    forward_blocks(sens, lhs, temp)
+    beside = functools.partial(
+        smooth_group, win=win, nb_ref=nb, small=small, offset=mine * (CELL_ROWS * 128), out=bent_out
+    )
+    forward_blocks(flipped, cols, d_all_out, temp, products, beside)
     hot = row_hot(rows)
     weight = data_weight[...]
-    predicted = sum_rows(hot, temp)
+    predicted = sum_rows(hot, products)
     weighted = (weight * weight * predicted).astype(BF16)
-    curvature = total(predicted * weighted.astype(F32)) + beta_reg * total(d_own * bent)
+    curvature = total(predicted * weighted.astype(F32)) + beta_reg * total(d_own * bent_out[...])
     backward_blocks(hot, weighted, slots, sens, lhs, spread)
     tail = scalar_tile(curvature)
     write_payload(out, spread, lambda o: tail)
@@ -280,6 +289,7 @@
 
 def scratch():
     return [
+        pltpu.VMEM((BLOCKS, 128), F32),
         pltpu.VMEM((BLOCKS, 128), F32),
         pltpu.VMEM((BLOCKS, 128), BF16),
         pltpu.VMEM((GROUP_DEVS * SLOTS, 128), F32),
@@ -310,30 +320,36 @@
     data_weight = data_weight.reshape(ROWS, 128)
     small = smallness.reshape(CELL_ROWS, 128)
     model = model.reshape(CELL_ROWS, 128)
-    diff = model - reference_model.reshape(CELL_ROWS, 128)
 
     def exchange(x):
         return lax.all_to_all(x, AXES, 0, 0, tiled=True)
 
-    payload = jnp.concatenate([model, diff[:8], diff[-8:]], axis=0).astype(BF16)
-    recv = exchange(jnp.broadcast_to(payload[None], (GROUP_DEVS, CELL_ROWS + 16, 128)))
+    diff, out = pl.pallas_call(
+        model_kernel,
+        out_shape=(cells_shape(), jax.ShapeDtypeStruct((GROUP_DEVS, CELL_ROWS + 16, 128), BF16)),
+        in_specs=[VM] * 2,
+        out_specs=(VM, VM),
+        compiler_params=PARAMS,
+        name="model",
+    )(model, reference_model.reshape(CELL_ROWS, 128))
+    recv = exchange(out)
     sent = jax.ShapeDtypeStruct((GROUP_DEVS, SENT_ROWS, 128), BF16)
     gather = jax.ShapeDtypeStruct((GROUP_DEVS, CELL_ROWS, 128), BF16)
-    out, bent = pl.pallas_call(
+    out, bent, kept, flipped = pl.pallas_call(
         start_kernel,
-        out_shape=(sent, cells_shape()),
+        out_shape=(sent, cells_shape(), pltpu.VMEM(sens.shape, BF16), pltpu.VMEM(sens.shape, BF16)),
         in_specs=[SM] * 3 + [pl.BlockSpec(memory_space=pltpu.HBM)] + [VM] * 8,
-        out_specs=(VM, VM),
+        out_specs=(VM,) * 4,
         scratch_shapes=scratch()
         + [
             pltpu.VMEM((TABLE, 128), F32),
-            pltpu.VMEM((BLOCKS, 128, 128), BF16),
             pltpu.SemaphoreType.DMA((BLOCKS // CHUNK,)),
         ],
-        compiler_params=pltpu.CompilerParams(vmem_limit_bytes=26 << 20),
+        compiler_params=pltpu.CompilerParams(vmem_limit_bytes=12 << 20),
         name="start",
     )(cols, slots, me, pltpu.with_memory_space_constraint(sens, pltpu.HBM), rows, recv, diff, observed, data_weight, nb, small, slot_hot)
-    sens = pltpu.with_memory_space_constraint(sens, pltpu.VMEM)
+    kept = pltpu.with_memory_space_constraint(kept, pltpu.VMEM)
+    flipped = pltpu.with_memory_space_constraint(flipped, pltpu.VMEM)
     residual, out, pick = pl.pallas_call(
         right_side_kernel,
         out_shape=(cells_shape(), gather, jax.ShapeDtypeStruct((CELL_ROWS, GROUP_DEVS * SLOTS), BF16)),
@@ -357,12 +373,12 @@
                 jax.ShapeDtypeStruct((TABLE, 128), F32),
                 jax.ShapeDtypeStruct((8, 128), F32),
             ),
-            in_specs=[SM] * 3 + [VM] * 10,
+            in_specs=[SM] * 3 + [VM] * 11,
             out_specs=(VM,) * 5,
             scratch_shapes=scratch(),
             compiler_params=PARAMS,
             name="step",
-        )(cols, slots, me, sens, rows, exchange(out), residual, direction, d_all, norm, data_weight, nb, small)
+        )(cols, slots, me, kept, flipped, rows, exchange(out), residual, direction, d_all, norm, data_weight, nb, small)
         results = pl.pallas_call(
             functools.partial(update_kernel, first, last),
             out_shape=(cells_shape(), cells_shape()) + (() if last else (gather,)),

time: 193 us -> 185 us (0.959)
  Pallas kernels: 46.4 us -> 36.9 us
  local copies, waits for them, and re-layouts: 1.15 us -> 4.51 us
    pallas_call x3, Pallas kernels: 33 us -> 21.9 us  [per_device(): pl.pallas_call(functools.partial(step_kernel, first), out_shape=(sent, ce...]
    unnamed x15 -> x19, local copies, waits for them, and re-layouts: 0.05 us -> 4.44 us
    pallas_call x1 -> x2, Pallas kernels: 11.6 us -> 13.1 us  [the longest x1 12.2 us: per_device(): pl.pallas_call(start_kernel, out_shape=(sent, cells_shape(), pltpu.VMEM(s...]
  transfers between devices with their start and end apart: 1 -> 1, of which waited for: 1 -> 1; matrix products, arithmetic and copies ran while one was open for 0% -> 1% of each run, Pallas kernels for 0% -> 0%
where the time goes in v3:
time: 185 us; the launch traced here: 184 us
  blocking collectives  115 us (62%)
  Pallas kernels  36.9 us (20%)
  waiting for transfers between devices  13.7 us (7%)
  starting transfers between devices  11.5 us (6%)
  local copies, waits for them, and re-layouts  4.51 us (2%)
    all_to_all x7, blocking collectives, exchange(): return lax.all_to_all(x, AXES, 0, 0, tiled=True)  115 us
    pallas_call x3, Pallas kernels, per_device(): pl.pallas_call(functools.partial(step_kernel, first), out_shape=(sent, ce...  21.9 us
    all_to_all x1, waiting for transfers between devices, exchange(): return lax.all_to_all(x, AXES, 0, 0, tiled=True)  13.7 us
    pallas_call x1, Pallas kernels, per_device(): pl.pallas_call(start_kernel, out_shape=(sent, cells_shape(), pltpu.VMEM(s...  12.2 us
    all_to_all x1, starting transfers between devices, exchange(): return lax.all_to_all(x, AXES, 0, 0, tiled=True)  11.5 us
    unnamed x19, local copies, waits for them, and re-layouts  4.44 us
  transfers between devices with their start and end apart: 1, of which 1 were waited for; matrix products, arithmetic and copies ran while one was open for 1% of the time, Pallas kernels for 0%

profile of v3, /device:TPU:0, one launch (start us, length us, event | category | flops | bytes accessed | tf_op | source)
XLA Modules:
  0.0 184.3 jit_solution(4740703000378197824)
XLA Ops:
  0.6 0.0 copy-start.4
  0.6 0.0 copy-start.3
  0.7 0.0 copy-start.2
  0.7 0.0 copy-start.6
  0.7 0.0 copy-start.5
  0.7 0.0 copy-start.7
  0.7 0.7 copy-done.7
  1.4 0.0 copy-start.8
  1.4 0.7 copy-done.8
  2.1 1.0 model.1
  3.1 11.5 %all-to-all-start = ((bf16[64,48,128]{2,1,0:T(8,128)(2,1)}), bf16[64,48,128]{2,1,0:T(8,128)(2,1)S(1)}, u32[]{:S(2)}, u32[]{:S(2)}) async-start(bf16[64,48,128]{2,1,0:T(8,128)(2,1)} %get-tuple-element.33), calls=%async_computation | async-start | bytes 1572864 | tf_op jit(solution)/shard_map/all_to_all | solution.py:325
  14.6 0.7 fusion.2
  15.3 0.2 convert_reduce_fusion
  15.6 0.3 select_reduce_fusion
  15.9 0.1 sub.14
  16.0 0.9 copy.13
  16.9 0.2 fusion.1.slot_hot
  17.1 13.7 %all-to-all-done.recv = bf16[64,48,128]{2,1,0:T(8,128)(2,1)S(1)} async-done(((bf16[64,48,128]{2,1,0:T(8,128)(2,1)}), bf16[64,48,128]{2,1,0:T(8,128)(2,1)S(1)}, u32[]{:S(2)}, u32[]{:S(2)}) %all-to-all-start) | async-done | bytes 786464 | tf_op jit(solution)/shard_map/all_to_all | solution.py:325
  30.8 0.0 copy-start
  30.8 0.9 copy-done
  31.7 0.0 copy-done.4
  31.7 0.0 copy-done.3
  31.7 0.0 copy-done.2
  31.7 0.0 copy-done.6
  31.7 0.0 copy-done.5
  31.7 0.0 copy-start.1
  31.7 1.1 copy-done.1
  32.9 12.2 %start.1 = (bf16[64,32,128]{2,1,0:T(8,128)(2,1)S(1)}, f32[32,128]{1,0:T(8,128)S(1)}, bf16[512,128,128]{2,1,0:T(8,128)(2,1)S(1)}, bf16[512,128,128]{2,1,0:T(8,128)(2,1)S(1)}) custom-call(s32[512]{0:T(512)S(1)} %copy-done.4, s32[512]{0:T(512)S(1)} %multiply_add_fusion.slots, s32[1]{0:T(128)} %bitcast.me, bf16[512,128,128]{2,1,0:T(8,128)(2,1)} %sens_hbm.1, ...), custom_call_target="tpu_custom_call" | custom-call | tf_op jit(solution)/shard_map/start/pallas_call | solution.py:338
  45.0 16.5 %all_to_all.40.recv = bf16[64,32,128]{2,1,0:T(8,128)(2,1)S(1)} all-to-all(bf16[64,32,128]{2,1,0:T(8,128)(2,1)S(1)} %get-tuple-element.37), channel_id=1, replica_groups=mesh['ref'=2,'lines'=8,'cells'=8] {'lines','cells'}, dimensions={0} | all-to-all | bytes 1048576 | tf_op jit(solution)/shard_map/all_to_all | solution.py:325
  61.5 0.3 right_side.1
  61.8 16.5 %all_to_all.41.recv = bf16[64,32,128]{2,1,0:T(8,128)(2,1)S(1)} all-to-all(bf16[64,32,128]{2,1,0:T(8,128)(2,1)S(1)} %get-tuple-element.39), channel_id=1, replica_groups=mesh['ref'=2,'lines'=8,'cells'=8] {'lines','cells'}, dimensions={0} | all-to-all | bytes 1048576 | tf_op jit(solution)/shard_map/all_to_all | solution.py:325
  78.3 6.8 %step.3 = (bf16[64,32,128]{2,1,0:T(8,128)(2,1)S(1)}, f32[32,128]{1,0:T(8,128)S(1)}, f32[32,128]{1,0:T(8,128)S(1)}, f32[2048,128]{1,0:T(8,128)S(1)}, f32[8,128]{1,0:T(8,128)S(1)}) custom-call(s32[512]{0:T(512)S(1)} %copy-done.4, s32[512]{0:T(512)S(1)} %multiply_add_fusion.slots, s32[1]{0:T(128)} %bitcast.me, ...), custom_call_target="tpu_custom_call" | custom-call | tf_op jit(solution)/shard_map/step/pallas_call | solution.py:367
  85.1 16.5 %all_to_all.42.recv = bf16[64,32,128]{2,1,0:T(8,128)(2,1)S(1)} all-to-all(bf16[64,32,128]{2,1,0:T(8,128)(2,1)S(1)} %get-tuple-element.41), channel_id=1, replica_groups=mesh['ref'=2,'lines'=8,'cells'=8] {'lines','cells'}, dimensions={0} | all-to-all | bytes 1048576 | tf_op jit(solution)/shard_map/all_to_all | solution.py:325
  101.6 0.3 update.3
  102.0 16.5 %all_to_all.43.recv = bf16[64,32,128]{2,1,0:T(8,128)(2,1)S(1)} all-to-all(bf16[64,32,128]{2,1,0:T(8,128)(2,1)S(1)} %get-tuple-element.46), channel_id=1, replica_groups=mesh['ref'=2,'lines'=8,'cells'=8] {'lines','cells'}, dimensions={0} | all-to-all | bytes 1048576 | tf_op jit(solution)/shard_map/all_to_all | solution.py:325
  118.5 7.1 %step.4 = (bf16[64,32,128]{2,1,0:T(8,128)(2,1)S(1)}, f32[32,128]{1,0:T(8,128)S(1)}, f32[32,128]{1,0:T(8,128)S(1)}, f32[2048,128]{1,0:T(8,128)S(1)}, f32[8,128]{1,0:T(8,128)S(1)}) custom-call(s32[512]{0:T(512)S(1)} %copy-done.4, s32[512]{0:T(512)S(1)} %multiply_add_fusion.slots, s32[1]{0:T(128)} %bitcast.me, ...), custom_call_target="tpu_custom_call" | custom-call | tf_op jit(solution)/shard_map/step/pallas_call | solution.py:367
  125.5 16.5 %all_to_all.44.recv = bf16[64,32,128]{2,1,0:T(8,128)(2,1)S(1)} all-to-all(bf16[64,32,128]{2,1,0:T(8,128)(2,1)S(1)} %get-tuple-element.49), channel_id=1, replica_groups=mesh['ref'=2,'lines'=8,'cells'=8] {'lines','cells'}, dimensions={0} | all-to-all | bytes 1048576 | tf_op jit(solution)/shard_map/all_to_all | solution.py:325
  142.0 0.3 update.4
  142.4 16.5 %all_to_all.45.recv = bf16[64,32,128]{2,1,0:T(8,128)(2,1)S(1)} all-to-all(bf16[64,32,128]{2,1,0:T(8,128)(2,1)S(1)} %get-tuple-element.54), channel_id=1, replica_groups=mesh['ref'=2,'lines'=8,'cells'=8] {'lines','cells'}, dimensions={0} | all-to-all | bytes 1048576 | tf_op jit(solution)/shard_map/all_to_all | solution.py:325
  158.9 8.1 %step.5 = (bf16[64,32,128]{2,1,0:T(8,128)(2,1)S(1)}, f32[32,128]{1,0:T(8,128)S(1)}, f32[32,128]{1,0:T(8,128)S(1)}, f32[2048,128]{1,0:T(8,128)}, f32[8,128]{1,0:T(8,128)S(1)}) custom-call(s32[512]{0:T(512)S(1)} %copy-done.4, s32[512]{0:T(512)S(1)} %multiply_add_fusion.slots, s32[1]{0:T(128)} %bitcast.me, bf16[512,128,128]{2,1,0:T(8,128)(2,1)S(1)} %get-tuple-element.35.sens, ...), custom_call_target="tpu_custom_call" | custom-call | tf_op jit(solution)/shard_map/step/pallas_call | solution.py:367
  166.9 16.5 %all_to_all.46.recv = bf16[64,32,128]{2,1,0:T(8,128)(2,1)S(1)} all-to-all(bf16[64,32,128]{2,1,0:T(8,128)(2,1)S(1)} %get-tuple-element.57), channel_id=1, replica_groups=mesh['ref'=2,'lines'=8,'cells'=8] {'lines','cells'}, dimensions={0} | all-to-all | bytes 1048576 | tf_op jit(solution)/shard_map/all_to_all | solution.py:325
  183.4 0.9 update.5
  (3 shorter events, 0.0 us)
Async XLA Ops:
  0.6 31.1 %copy-start.4 = (s32[512]{0:T(512)S(1)}, s32[512]{0:T(512)}, u32[]{:S(2)}) copy-start(s32[512]{0:T(512)} %cols.7) | copy-start | bytes 6148
  0.6 31.1 %copy-start.3 = (f32[4096]{0:T(1024)S(1)}, f32[4096]{0:T(1024)}, u32[]{:S(2)}) copy-start(f32[4096]{0:T(1024)} %param.15) | copy-start | bytes 49156
  0.7 31.1 %copy-start.2 = (f32[4096]{0:T(1024)S(1)}, f32[4096]{0:T(1024)}, u32[]{:S(2)}) copy-start(f32[4096]{0:T(1024)} %param.14) | copy-start | bytes 49156
  0.7 31.1 %copy-start.6 = (f32[4096]{0:T(1024)S(1)}, f32[4096]{0:T(1024)}, u32[]{:S(2)}) copy-start(f32[4096]{0:T(1024)} %param.13) | copy-start | bytes 49156
  0.7 31.1 %copy-start.5 = (s32[512]{0:T(512)S(1)}, s32[512]{0:T(512)}, u32[]{:S(2)}) copy-start(s32[512]{0:T(512)} %param.10) | copy-start | bytes 6148
  0.7 0.7 copy-start.7
  1.4 0.7 copy-start.8
  3.1 27.7 %all-to-all-start = ((bf16[64,48,128]{2,1,0:T(8,128)(2,1)}), bf16[64,48,128]{2,1,0:T(8,128)(2,1)S(1)}, u32[]{:S(2)}, u32[]{:S(2)}) async-start(bf16[64,48,128]{2,1,0:T(8,128)(2,1)} %get-tuple-element.33), calls=%async_computation | async-start | bytes 1572864 | tf_op jit(solution)/shard_map/all_to_all | solution.py:325
  30.8 0.9 copy-start
  31.7 1.1 copy-start.1

commit v4 on v3

--- a/solution.py
+++ b/solution.py
@@ -12,15 +12,16 @@
 
 AXES = ("lines", "cells")
 BLOCKS = 512
-CHUNK = 128
+CHUNK = 256
+START_CHUNK = 256
+PARTS = BLOCKS // START_CHUNK
 BATCH = 16
 GROUP_DEVS = 64
 ROWS = 32
 CELL_ROWS = 32
 TABLE = GROUP_DEVS * CELL_ROWS
 SLOTS = 16
-EXTRA = 16
-SENT_ROWS = SLOTS + EXTRA
+EXTRA = 8
 F32 = jnp.float32
 BF16 = jnp.bfloat16
 
@@ -49,13 +50,17 @@
 
 
 def forward_blocks(flipped, cols, tab, temp, products, beside, flip=None):
+    size = CHUNK if flip is None else START_CHUNK
+    pieces = CELL_ROWS // 8 * size // BLOCKS
+
     def chunk(g, _):
-        first = pl.multiple_of(g * CHUNK, CHUNK)
+        first = pl.multiple_of(g * size, size)
         if flip is not None:
             sens, wait = flip
             wait(g)
-        beside(g)
-        for h in range(CHUNK // BATCH):
+        for piece in range(pieces):
+            beside(g * pieces + piece)
+        for h in range(size // BATCH):
             base = first + h * BATCH
             for q in range(BATCH):
                 temp[pl.ds(base + q, 1), :] = tab[pl.ds(cols[base + q], 1), :]
@@ -71,7 +76,7 @@
                 products[pl.ds(base + q, 1), :] = out[q : q + 1, q * 128 : (q + 1) * 128]
         return 0
 
-    lax.fori_loop(0, BLOCKS // CHUNK, chunk, 0)
+    lax.fori_loop(0, BLOCKS // size, chunk, 0)
 
 
 def row_hot(rows):
@@ -119,7 +124,7 @@
     place = sub * 128 + lane
     return jnp.where(
         place == 0, high, jnp.where(place == 1, middle, jnp.where(place == 2, low, 0.0))
-    ).astype(BF16)
+    )
 
 
 def write_payload(out, spread, tail_of):
@@ -127,36 +132,54 @@
         for q in range(8):
             o = g * 8 + q
             base = pl.multiple_of(o * SLOTS, SLOTS)
-            out[o, pl.ds(0, SLOTS), :] = spread[pl.ds(base, SLOTS), :].astype(BF16)
-            out[o, pl.ds(SLOTS, EXTRA), :] = tail_of(o)
+            out[o] = jnp.concatenate([spread[pl.ds(base, SLOTS), :], tail_of(o)], axis=0).astype(BF16)
         return 0
 
     lax.fori_loop(0, GROUP_DEVS // 8, owners, 0)
 
 
-def model_kernel(model, reference_model, diff_out, out):
+def model_kernel(model_hbm, reference_hbm, diff_out, out, model, reference_model, half, sems):
+    first = pltpu.make_async_copy(model_hbm, model, sems.at[0])
+    second = pltpu.make_async_copy(reference_hbm, reference_model, sems.at[1])
+    first.start()
+    second.start()
+    first.wait()
+    second.wait()
     diff = model[...] - reference_model[...]
     diff_out[...] = diff
-    half = jnp.concatenate([model[...], diff[:8], diff[-8:]], axis=0).astype(BF16)
-
-    def owners(g, _):
-        for q in range(8):
-            out[g * 8 + q] = half
-        return 0
-
-    lax.fori_loop(0, GROUP_DEVS // 8, owners, 0)
+    payload = jnp.concatenate([model[...], diff[:8], diff[-8:]], axis=0).astype(BF16)
+    for q in range(8):
+        half[q] = payload
+    sends = [
+        pltpu.make_async_copy(half, out.at[pl.ds(8 * g, 8)], sems.at[2 + g]) for g in range(GROUP_DEVS // 8)
+    ]
+    for send in sends:
+        send.start()
+    for send in sends:
+        send.wait()
 
 
 def start_kernel(
-    cols, slots, me, sens_hbm, rows, recv, diff, observed, data_weight, nb, small, slot_hot,
-    out, bent_out, sens, flipped, temp, products, lhs, spread, win, tab, sems,
+    cols, slots, me, sens_hbm, recv, *refs,
 ):
+    given, (out, bent_out, sens, flipped), held = refs[:7], refs[7:11], refs[11:18]
+    temp, products, lhs, spread, win, tab, sems, held_sems = refs[18:]
+    diff, small, nb, rows, observed, data_weight, slot_hot = held
+    copies = [
+        pltpu.make_async_copy(source, target, held_sems.at[i])
+        for i, (source, target) in enumerate(zip(given, held))
+    ]
+    for copy in copies:
+        copy.start()
+
     def part(g):
-        span = pl.ds(pl.multiple_of(g * CHUNK, CHUNK), CHUNK)
+        span = pl.ds(pl.multiple_of(g * START_CHUNK, START_CHUNK), START_CHUNK)
         return pltpu.make_async_copy(sens_hbm.at[span], sens.at[span], sems.at[g])
 
-    for g in range(BLOCKS // CHUNK):
+    for g in range(PARTS):
         part(g).start()
+    for copy in copies:
+        copy.wait()
 
     def owners(g, _):
         for q in range(8):
@@ -180,13 +203,13 @@
     weight = data_weight[...]
     misfit = weight * weight * (sum_rows(hot, products) - observed[...])
     backward_blocks(hot, misfit.astype(BF16), slots, sens, lhs, spread)
-    write_payload(out, spread, lambda o: slot_hot[o])
+    write_payload(out, spread, lambda o: slot_hot[o].astype(F32))
 
 
 def step_kernel(
     first_step,
     cols, slots, me, sens, flipped, rows, recv, residual, direction, d_all_in, norm_in, data_weight, nb, small,
-    out, bent_out, d_out, d_all_out, norm_out, temp, products, lhs, spread, win,
+    out, bent_out, d_out, norm_out, d_all_out, temp, products, lhs, spread, win,
 ):
     def squares(g, acc):
         for q in range(8):
@@ -252,7 +275,7 @@
 
 
 def right_side_kernel(recv, bent, r_out, out, pick_out):
-    hot = recv[:, SLOTS : SLOTS + EXTRA, :].reshape(GROUP_DEVS * SLOTS, 128)
+    hot = recv[:, SLOTS : 2 * SLOTS, :].reshape(GROUP_DEVS * SLOTS, 128)
     pick = hot.astype(F32).T[:CELL_ROWS].astype(BF16)
     pick_out[...] = pick
     r = -(gathered_sum(recv, pick) + beta_reg * bent[...])
@@ -265,7 +288,7 @@
 
     def tails(g, acc):
         for q in range(8):
-            acc = acc + recv[g * 8 + q, pl.ds(SLOTS, EXTRA), :].astype(F32)
+            acc = acc + recv[g * 8 + q].astype(F32)[SLOTS:]
         return acc
 
     curvature = total(lax.fori_loop(0, GROUP_DEVS // 8, tails, jnp.zeros((EXTRA, 128), F32)))
@@ -280,7 +303,12 @@
 
 VM = pl.BlockSpec(memory_space=pltpu.VMEM)
 SM = pl.BlockSpec(memory_space=pltpu.SMEM)
+HB = pl.BlockSpec(memory_space=pltpu.HBM)
 PARAMS = pltpu.CompilerParams(vmem_limit_bytes=12 << 20)
+
+
+def in_hbm(x):
+    return pltpu.with_memory_space_constraint(x, pltpu.HBM)
 
 
 def cells_shape():
@@ -326,28 +354,35 @@
 
     diff, out = pl.pallas_call(
         model_kernel,
-        out_shape=(cells_shape(), jax.ShapeDtypeStruct((GROUP_DEVS, CELL_ROWS + 16, 128), BF16)),
-        in_specs=[VM] * 2,
-        out_specs=(VM, VM),
+        out_shape=(cells_shape(), pltpu.HBM((GROUP_DEVS, CELL_ROWS + 16, 128), BF16)),
+        in_specs=[HB] * 2,
+        out_specs=(VM, HB),
+        scratch_shapes=[pltpu.VMEM((CELL_ROWS, 128), F32)] * 2
+        + [pltpu.VMEM((8, CELL_ROWS + 16, 128), BF16), pltpu.SemaphoreType.DMA((2 + GROUP_DEVS // 8,))],
         compiler_params=PARAMS,
         name="model",
-    )(model, reference_model.reshape(CELL_ROWS, 128))
+    )(in_hbm(model), in_hbm(reference_model.reshape(CELL_ROWS, 128)))
     recv = exchange(out)
-    sent = jax.ShapeDtypeStruct((GROUP_DEVS, SENT_ROWS, 128), BF16)
+    def sent(rows):
+        return jax.ShapeDtypeStruct((GROUP_DEVS, SLOTS + rows, 128), BF16)
+
     gather = jax.ShapeDtypeStruct((GROUP_DEVS, CELL_ROWS, 128), BF16)
+    given = (diff, small, nb, rows, observed, data_weight, slot_hot)
     out, bent, kept, flipped = pl.pallas_call(
         start_kernel,
-        out_shape=(sent, cells_shape(), pltpu.VMEM(sens.shape, BF16), pltpu.VMEM(sens.shape, BF16)),
-        in_specs=[SM] * 3 + [pl.BlockSpec(memory_space=pltpu.HBM)] + [VM] * 8,
+        out_shape=(sent(SLOTS), cells_shape(), pltpu.VMEM(sens.shape, BF16), pltpu.VMEM(sens.shape, BF16)),
+        in_specs=[SM] * 3 + [HB, VM] + [HB] * 7,
         out_specs=(VM,) * 4,
-        scratch_shapes=scratch()
+        scratch_shapes=[pltpu.VMEM(x.shape, x.dtype) for x in given]
+        + scratch()
         + [
             pltpu.VMEM((TABLE, 128), F32),
-            pltpu.SemaphoreType.DMA((BLOCKS // CHUNK,)),
+            pltpu.SemaphoreType.DMA((PARTS,)),
+            pltpu.SemaphoreType.DMA((len(given),)),
         ],
-        compiler_params=pltpu.CompilerParams(vmem_limit_bytes=12 << 20),
+        compiler_params=PARAMS,
         name="start",
-    )(cols, slots, me, pltpu.with_memory_space_constraint(sens, pltpu.HBM), rows, recv, diff, observed, data_weight, nb, small, slot_hot)
+    )(cols, slots, me, in_hbm(sens), recv, *[in_hbm(x) for x in given])
     kept = pltpu.with_memory_space_constraint(kept, pltpu.VMEM)
     flipped = pltpu.with_memory_space_constraint(flipped, pltpu.VMEM)
     residual, out, pick = pl.pallas_call(
@@ -364,18 +399,18 @@
     norm = jnp.zeros((8, 128), F32)
     for step in range(CG_STEPS):
         first, last = step == 0, step == CG_STEPS - 1
-        out, bent, direction, d_all, norm = pl.pallas_call(
+        out, bent, direction, norm, *tables = pl.pallas_call(
             functools.partial(step_kernel, first),
             out_shape=(
-                sent,
+                sent(EXTRA),
                 cells_shape(),
                 cells_shape(),
-                jax.ShapeDtypeStruct((TABLE, 128), F32),
                 jax.ShapeDtypeStruct((8, 128), F32),
-            ),
+            )
+            + (() if last else (jax.ShapeDtypeStruct((TABLE, 128), F32),)),
             in_specs=[SM] * 3 + [VM] * 11,
-            out_specs=(VM,) * 5,
-            scratch_shapes=scratch(),
+            out_specs=(VM,) * (4 if last else 5),
+            scratch_shapes=([pltpu.VMEM((TABLE, 128), F32)] if last else []) + scratch(),
             compiler_params=PARAMS,
             name="step",
         )(cols, slots, me, kept, flipped, rows, exchange(out), residual, direction, d_all, norm, data_weight, nb, small)
@@ -389,6 +424,7 @@
         )(exchange(out), pick, bent, direction, residual, update, norm)
         update, residual = results[:2]
         if not last:
+            d_all = tables[0]
             out = results[2]
     return update.reshape(-1), residual.reshape(-1)
 

time: 185 us -> 180 us (0.973)
  local copies, waits for them, and re-layouts: 4.51 us -> 2.26 us
    unnamed x19 -> x13, local copies, waits for them, and re-layouts: 4.44 us -> 2.19 us
  transfers between devices with their start and end apart: 1 -> 1, of which waited for: 1 -> 1; matrix products, arithmetic and copies ran while one was open for 1% -> 2% of each run, Pallas kernels for 0% -> 0%
where the time goes in v4:
time: 180 us; the launch traced here: 179 us
  blocking collectives  114 us (63%)
  Pallas kernels  36.2 us (20%)
  waiting for transfers between devices  12.4 us (7%)
  starting transfers between devices  11.5 us (6%)
  local copies, waits for them, and re-layouts  2.26 us (1%)
  other arithmetic  2.16 us (1%)
    all_to_all x7, blocking collectives, exchange(): return lax.all_to_all(x, AXES, 0, 0, tiled=True)  114 us
    pallas_call x3, Pallas kernels, per_device(): pl.pallas_call(functools.partial(step_kernel, first), out_shape=(sent(EXT...  19.6 us
    pallas_call x1, Pallas kernels, per_device(): pl.pallas_call(start_kernel, out_shape=(sent(SLOTS), cells_shape(), pltpu...  13 us
    all_to_all x1, waiting for transfers between devices, exchange(): return lax.all_to_all(x, AXES, 0, 0, tiled=True)  12.4 us
    all_to_all x1, starting transfers between devices, exchange(): return lax.all_to_all(x, AXES, 0, 0, tiled=True)  11.5 us
  transfers between devices with their start and end apart: 1, of which 1 were waited for; matrix products, arithmetic and copies ran while one was open for 2% of the time, Pallas kernels for 0%

profile of v4, /device:TPU:0, one launch (start us, length us, event | category | flops | bytes accessed | tf_op | source)
XLA Modules:
  0.0 179.1 jit_solution(2388425674836396571)
XLA Ops:
  0.6 0.0 copy-start.3
  0.6 1.7 model.1
  2.4 0.0 copy-start.5
  2.4 0.6 copy-done.5
  3.0 11.5 %all-to-all-start = ((bf16[64,48,128]{2,1,0:T(8,128)(2,1)}), bf16[64,48,128]{2,1,0:T(8,128)(2,1)S(1)}, u32[]{:S(2)}, u32[]{:S(2)}) async-start(bf16[64,48,128]{2,1,0:T(8,128)(2,1)} %get-tuple-element.33), calls=%async_computation | async-start | bytes 1572864 | tf_op jit(solution)/shard_map/all_to_all | solution.py:353
  14.5 0.7 fusion.2
  15.2 0.2 convert_reduce_fusion
  15.4 0.3 select_reduce_fusion
  15.8 0.1 sub.14
  15.8 1.6 copy.13
  17.4 0.9 fusion.1.refs_6_
  18.3 12.4 %all-to-all-done.recv = bf16[64,48,128]{2,1,0:T(8,128)(2,1)S(1)} async-done(((bf16[64,48,128]{2,1,0:T(8,128)(2,1)}), bf16[64,48,128]{2,1,0:T(8,128)(2,1)S(1)}, u32[]{:S(2)}, u32[]{:S(2)}) %all-to-all-start) | async-done | bytes 786464 | tf_op jit(solution)/shard_map/all_to_all | solution.py:353
  30.7 0.0 copy-done.3
  30.7 13.0 %start.1 = (bf16[64,32,128]{2,1,0:T(8,128)(2,1)S(1)}, f32[32,128]{1,0:T(8,128)S(1)}, bf16[512,128,128]{2,1,0:T(8,128)(2,1)S(1)}, bf16[512,128,128]{2,1,0:T(8,128)(2,1)S(1)}) custom-call(s32[512]{0:T(512)S(1)} %copy-done.3, s32[512]{0:T(512)S(1)} %multiply_add_fusion.slots, s32[1]{0:T(128)} %bitcast.me, bf16[512,128,128]{2,1,0:T(8,128)(2,1)} %sens_hbm.1, ...), custom_call_target="tpu_custom_call" | custom-call | tf_op jit(solution)/shard_map/start/pallas_call | solution.py:371
  43.7 0.0 copy-start
  43.7 0.0 copy-start.1
  43.7 0.0 copy-start.2
  43.7 0.0 copy-start.4
  43.7 16.6 %all_to_all.40.recv = bf16[64,32,128]{2,1,0:T(8,128)(2,1)S(1)} all-to-all(bf16[64,32,128]{2,1,0:T(8,128)(2,1)S(1)} %get-tuple-element.37), channel_id=1, replica_groups=mesh['ref'=2,'lines'=8,'cells'=8] {'lines','cells'}, dimensions={0} | all-to-all | bytes 1048576 | tf_op jit(solution)/shard_map/all_to_all | solution.py:353
  60.3 0.3 right_side.1
  60.6 16.5 %all_to_all.41.recv = bf16[64,32,128]{2,1,0:T(8,128)(2,1)S(1)} all-to-all(bf16[64,32,128]{2,1,0:T(8,128)(2,1)S(1)} %get-tuple-element.39), channel_id=1, replica_groups=mesh['ref'=2,'lines'=8,'cells'=8] {'lines','cells'}, dimensions={0} | all-to-all | bytes 1048576 | tf_op jit(solution)/shard_map/all_to_all | solution.py:353
  77.1 0.0 copy-done
  77.1 0.0 copy-done.1
  77.1 0.0 copy-done.2
  77.1 0.0 copy-done.4
  77.1 6.4 %step.3 = (bf16[64,24,128]{2,1,0:T(8,128)(2,1)S(1)}, f32[32,128]{1,0:T(8,128)S(1)}, f32[32,128]{1,0:T(8,128)S(1)}, f32[8,128]{1,0:T(8,128)S(1)}, f32[2048,128]{1,0:T(8,128)S(1)}) custom-call(s32[512]{0:T(512)S(1)} %copy-done.3, s32[512]{0:T(512)S(1)} %multiply_add_fusion.slots, s32[1]{0:T(128)} %bitcast.me, ...), custom_call_target="tpu_custom_call" | custom-call | tf_op jit(solution)/shard_map/step/pallas_call | solution.py:402
  83.5 15.8 %all_to_all.42.recv = bf16[64,24,128]{2,1,0:T(8,128)(2,1)S(1)} all-to-all(bf16[64,24,128]{2,1,0:T(8,128)(2,1)S(1)} %get-tuple-element.41), channel_id=1, replica_groups=mesh['ref'=2,'lines'=8,'cells'=8] {'lines','cells'}, dimensions={0} | all-to-all | bytes 786432 | tf_op jit(solution)/shard_map/all_to_all | solution.py:353
  99.3 0.3 update.3
  99.7 16.8 %all_to_all.43.recv = bf16[64,32,128]{2,1,0:T(8,128)(2,1)S(1)} all-to-all(bf16[64,32,128]{2,1,0:T(8,128)(2,1)S(1)} %get-tuple-element.46), channel_id=1, replica_groups=mesh['ref'=2,'lines'=8,'cells'=8] {'lines','cells'}, dimensions={0} | all-to-all | bytes 1048576 | tf_op jit(solution)/shard_map/all_to_all | solution.py:353
  116.4 6.6 %step.4 = (bf16[64,24,128]{2,1,0:T(8,128)(2,1)S(1)}, f32[32,128]{1,0:T(8,128)S(1)}, f32[32,128]{1,0:T(8,128)S(1)}, f32[8,128]{1,0:T(8,128)S(1)}, f32[2048,128]{1,0:T(8,128)S(1)}) custom-call(s32[512]{0:T(512)S(1)} %copy-done.3, s32[512]{0:T(512)S(1)} %multiply_add_fusion.slots, s32[1]{0:T(128)} %bitcast.me, ...), custom_call_target="tpu_custom_call" | custom-call | tf_op jit(solution)/shard_map/step/pallas_call | solution.py:402
  123.1 15.8 %all_to_all.44.recv = bf16[64,24,128]{2,1,0:T(8,128)(2,1)S(1)} all-to-all(bf16[64,24,128]{2,1,0:T(8,128)(2,1)S(1)} %get-tuple-element.49), channel_id=1, replica_groups=mesh['ref'=2,'lines'=8,'cells'=8] {'lines','cells'}, dimensions={0} | all-to-all | bytes 786432 | tf_op jit(solution)/shard_map/all_to_all | solution.py:353
  138.9 0.3 update.4
  139.2 16.6 %all_to_all.45.recv = bf16[64,32,128]{2,1,0:T(8,128)(2,1)S(1)} all-to-all(bf16[64,32,128]{2,1,0:T(8,128)(2,1)S(1)} %get-tuple-element.54), channel_id=1, replica_groups=mesh['ref'=2,'lines'=8,'cells'=8] {'lines','cells'}, dimensions={0} | all-to-all | bytes 1048576 | tf_op jit(solution)/shard_map/all_to_all | solution.py:353
  155.8 6.6 %step.5 = (bf16[64,24,128]{2,1,0:T(8,128)(2,1)S(1)}, f32[32,128]{1,0:T(8,128)S(1)}, f32[32,128]{1,0:T(8,128)S(1)}, f32[8,128]{1,0:T(8,128)S(1)}) custom-call(s32[512]{0:T(512)S(1)} %copy-done.3, s32[512]{0:T(512)S(1)} %multiply_add_fusion.slots, s32[1]{0:T(128)} %bitcast.me, bf16[512,128,128]{2,1,0:T(8,128)(2,1)S(1)} %get-tuple-element.35.sens, ...), custom_call_target="tpu_custom_call" | custom-call | tf_op jit(solution)/shard_map/step/pallas_call | solution.py:402
  162.4 15.8 %all_to_all.46.recv = bf16[64,24,128]{2,1,0:T(8,128)(2,1)S(1)} all-to-all(bf16[64,24,128]{2,1,0:T(8,128)(2,1)S(1)} %get-tuple-element.57), channel_id=1, replica_groups=mesh['ref'=2,'lines'=8,'cells'=8] {'lines','cells'}, dimensions={0} | all-to-all | bytes 786432 | tf_op jit(solution)/shard_map/all_to_all | solution.py:353
  178.2 0.9 update.5
  (3 shorter events, 0.0 us)
Async XLA Ops:
  0.6 30.0 %copy-start.3 = (s32[512]{0:T(512)S(1)}, s32[512]{0:T(512)}, u32[]{:S(2)}) copy-start(s32[512]{0:T(512)} %cols.7) | copy-start | bytes 6148
  2.4 0.6 copy-start.5
  3.0 27.7 %all-to-all-start = ((bf16[64,48,128]{2,1,0:T(8,128)(2,1)}), bf16[64,48,128]{2,1,0:T(8,128)(2,1)S(1)}, u32[]{:S(2)}, u32[]{:S(2)}) async-start(bf16[64,48,128]{2,1,0:T(8,128)(2,1)} %get-tuple-element.33), calls=%async_computation | async-start | bytes 1572864 | tf_op jit(solution)/shard_map/all_to_all | solution.py:353
  43.7 33.5 %copy-start = (s32[1,6,32,128]{3,2,1,0:T(8,128)S(1)}, s32[1,6,32,128]{3,2,1,0:T(8,128)}, u32[]{:S(2)}) copy-start(s32[1,6,32,128]{3,2,1,0:T(8,128)} %copy.13) | copy-start | bytes 294916
  43.7 33.5 %copy-start.1 = (f32[4096]{0:T(1024)S(1)}, f32[4096]{0:T(1024)}, u32[]{:S(2)}) copy-start(f32[4096]{0:T(1024)} %param.15) | copy-start | bytes 49156
  43.7 33.4 %copy-start.2 = (f32[4096]{0:T(1024)S(1)}, f32[4096]{0:T(1024)}, u32[]{:S(2)}) copy-start(f32[4096]{0:T(1024)} %param.14) | copy-start | bytes 49156
  43.7 33.4 %copy-start.4 = (s32[512]{0:T(512)S(1)}, s32[512]{0:T(512)}, u32[]{:S(2)}) copy-start(s32[512]{0:T(512)} %param.10) | copy-start | bytes 6148

commit v5 on v4

--- a/solution.py
+++ b/solution.py
@@ -12,7 +12,7 @@
 
 AXES = ("lines", "cells")
 BLOCKS = 512
-CHUNK = 256
+CHUNK = 512
 START_CHUNK = 256
 PARTS = BLOCKS // START_CHUNK
 BATCH = 16
@@ -164,7 +164,7 @@
 ):
     given, (out, bent_out, sens, flipped), held = refs[:7], refs[7:11], refs[11:18]
     temp, products, lhs, spread, win, tab, sems, held_sems = refs[18:]
-    diff, small, nb, rows, observed, data_weight, slot_hot = held
+    diff, small, nb, rows, observed, data_weight, slot_cells = held
     copies = [
         pltpu.make_async_copy(source, target, held_sems.at[i])
         for i, (source, target) in enumerate(zip(given, held))
@@ -203,7 +203,7 @@
     weight = data_weight[...]
     misfit = weight * weight * (sum_rows(hot, products) - observed[...])
     backward_blocks(hot, misfit.astype(BF16), slots, sens, lhs, spread)
-    write_payload(out, spread, lambda o: slot_hot[o].astype(F32))
+    write_payload(out, spread, lambda o: slot_cells[o])
 
 
 def step_kernel(
@@ -274,9 +274,26 @@
     lax.fori_loop(0, GROUP_DEVS // 8, owners, 0)
 
 
-def right_side_kernel(recv, bent, r_out, out, pick_out):
-    hot = recv[:, SLOTS : 2 * SLOTS, :].reshape(GROUP_DEVS * SLOTS, 128)
-    pick = hot.astype(F32).T[:CELL_ROWS].astype(BF16)
+def right_side_kernel(recv, bent, r_out, out, pick_out, cells):
+    def owners(g, _):
+        for q in range(8):
+            o = g * 8 + q
+            cells[pl.ds(o, 1), :] = recv[o].astype(F32)[SLOTS : SLOTS + 1]
+        return 0
+
+    lax.fori_loop(0, GROUP_DEVS // 8, owners, 0)
+    width = GROUP_DEVS * SLOTS
+    spread = (
+        lax.broadcasted_iota(jnp.int32, (128, width), 1) % SLOTS
+        == lax.broadcasted_iota(jnp.int32, (128, width), 0)
+    ).astype(BF16)
+    everywhere = jnp.dot(cells[...].astype(BF16), spread, preferred_element_type=F32)
+    mine = (
+        lax.broadcasted_iota(jnp.int32, (GROUP_DEVS, width), 1) // SLOTS
+        == lax.broadcasted_iota(jnp.int32, (GROUP_DEVS, width), 0)
+    )
+    cell = jnp.sum(jnp.where(mine, everywhere, 0.0), axis=0, keepdims=True).astype(jnp.int32)
+    pick = (lax.broadcasted_iota(jnp.int32, (CELL_ROWS, width), 0) == cell).astype(BF16)
     pick_out[...] = pick
     r = -(gathered_sum(recv, pick) + beta_reg * bent[...])
     r_out[...] = r
@@ -332,15 +349,15 @@
     slots = owners * SLOTS + jnp.sum(shared.astype(jnp.int32), axis=1)
     taken = slots[None, :] == jnp.arange(GROUP_DEVS * SLOTS, dtype=jnp.int32)[:, None]
     cell = jnp.sum(jnp.where(taken, (block_cols % CELL_ROWS)[None, :] + 1, 0), axis=1) - 1
-    hot = (cell[:, None] == jnp.arange(128, dtype=jnp.int32)[None, :]).astype(BF16)
-    return slots, hot.reshape(GROUP_DEVS, SLOTS, 128)
+    cell = jnp.maximum(cell, 0).astype(F32).reshape(GROUP_DEVS, 1, SLOTS)
+    return slots, jnp.pad(cell, ((0, 0), (0, EXTRA - 1), (0, 128 - SLOTS)))
 
 
 def per_device(
     sens, block_rows, block_cols, neighbours, observed, data_weight, smallness, model, reference_model
 ):
     cols = block_cols
-    slots, slot_hot = slot_lists(block_cols)
+    slots, slot_cells = slot_lists(block_cols)
     rows = block_rows.reshape(1, BLOCKS)
     me = lax.axis_index(AXES).astype(jnp.int32).reshape(1)
     nb = neighbours.reshape(6, CELL_ROWS, 128)
@@ -367,10 +384,10 @@
         return jax.ShapeDtypeStruct((GROUP_DEVS, SLOTS + rows, 128), BF16)
 
     gather = jax.ShapeDtypeStruct((GROUP_DEVS, CELL_ROWS, 128), BF16)
-    given = (diff, small, nb, rows, observed, data_weight, slot_hot)
+    given = (diff, small, nb, rows, observed, data_weight, slot_cells)
     out, bent, kept, flipped = pl.pallas_call(
         start_kernel,
-        out_shape=(sent(SLOTS), cells_shape(), pltpu.VMEM(sens.shape, BF16), pltpu.VMEM(sens.shape, BF16)),
+        out_shape=(sent(EXTRA), cells_shape(), pltpu.VMEM(sens.shape, BF16), pltpu.VMEM(sens.shape, BF16)),
         in_specs=[SM] * 3 + [HB, VM] + [HB] * 7,
         out_specs=(VM,) * 4,
         scratch_shapes=[pltpu.VMEM(x.shape, x.dtype) for x in given]
@@ -390,6 +407,7 @@
         out_shape=(cells_shape(), gather, jax.ShapeDtypeStruct((CELL_ROWS, GROUP_DEVS * SLOTS), BF16)),
         in_specs=[VM] * 2,
         out_specs=(VM,) * 3,
+        scratch_shapes=[pltpu.VMEM((GROUP_DEVS, 128), F32)],
         compiler_params=PARAMS,
         name="right_side",
     )(exchange(out), bent)

time: 180 us -> 178 us (0.989)
  no operation moved by 1% of the time
where the time goes in v5:
time: 178 us
  blocking collectives  113 us (63%)
  Pallas kernels  35.4 us (20%)
  waiting for transfers between devices  12.5 us (7%)
  starting transfers between devices  11.5 us (6%)
  local copies, waits for them, and re-layouts  3 us (2%)
    all_to_all x7, blocking collectives, exchange(): return lax.all_to_all(x, AXES, 0, 0, tiled=True)  113 us
    pallas_call x3, Pallas kernels, per_device(): pl.pallas_call(functools.partial(step_kernel, first), out_shape=(sent(EXT...  18.9 us
    pallas_call x1, Pallas kernels, per_device(): pl.pallas_call(start_kernel, out_shape=(sent(EXTRA), cells_shape(), pltpu...  12.8 us
    all_to_all x1, waiting for transfers between devices, exchange(): return lax.all_to_all(x, AXES, 0, 0, tiled=True)  12.5 us
    all_to_all x1, starting transfers between devices, exchange(): return lax.all_to_all(x, AXES, 0, 0, tiled=True)  11.5 us
  transfers between devices with their start and end apart: 1, of which 1 were waited for; matrix products, arithmetic and copies ran while one was open for 2% of the time, Pallas kernels for 0%

profile of v5, /device:TPU:0, one launch (start us, length us, event | category | flops | bytes accessed | tf_op | source)
XLA Modules:
  0.0 177.7 jit_solution(6900133291243426856)
XLA Ops:
  0.6 0.0 copy-start.3
  0.6 1.7 model.1
  2.4 0.0 copy-start.5
  2.4 0.6 copy-done.5
  3.0 11.5 %all-to-all-start = ((bf16[64,48,128]{2,1,0:T(8,128)(2,1)}), bf16[64,48,128]{2,1,0:T(8,128)(2,1)S(1)}, u32[]{:S(2)}, u32[]{:S(2)}) async-start(bf16[64,48,128]{2,1,0:T(8,128)(2,1)} %get-tuple-element.33), calls=%async_computation | async-start | bytes 1572864 | tf_op jit(solution)/shard_map/all_to_all | solution.py:370
  14.5 0.7 fusion.1
  15.2 0.2 convert_reduce_fusion
  15.4 0.3 select_reduce_fusion
  15.7 0.1 convert_element_type.20
  15.8 1.6 copy.15
  17.4 0.7 pad.4.refs_6_
  18.1 12.5 %all-to-all-done.recv = bf16[64,48,128]{2,1,0:T(8,128)(2,1)S(1)} async-done(((bf16[64,48,128]{2,1,0:T(8,128)(2,1)}), bf16[64,48,128]{2,1,0:T(8,128)(2,1)S(1)}, u32[]{:S(2)}, u32[]{:S(2)}) %all-to-all-start) | async-done | bytes 786464 | tf_op jit(solution)/shard_map/all_to_all | solution.py:370
  30.7 0.0 copy-done.3
  30.7 12.8 %start.1 = (bf16[64,24,128]{2,1,0:T(8,128)(2,1)S(1)}, f32[32,128]{1,0:T(8,128)S(1)}, bf16[512,128,128]{2,1,0:T(8,128)(2,1)S(1)}, bf16[512,128,128]{2,1,0:T(8,128)(2,1)S(1)}) custom-call(s32[512]{0:T(512)S(1)} %copy-done.3, s32[512]{0:T(512)S(1)} %multiply_add_fusion.slots, s32[1]{0:T(128)} %bitcast.me, bf16[512,128,128]{2,1,0:T(8,128)(2,1)} %sens_hbm.1, ...), custom_call_target="tpu_custom_call" | custom-call | tf_op jit(solution)/shard_map/start/pallas_call | solution.py:388
  43.5 0.0 copy-start
  43.5 0.0 copy-start.1
  43.5 0.0 copy-start.2
  43.6 0.0 copy-start.4
  43.6 15.8 %all_to_all.40.recv = bf16[64,24,128]{2,1,0:T(8,128)(2,1)S(1)} all-to-all(bf16[64,24,128]{2,1,0:T(8,128)(2,1)S(1)} %get-tuple-element.37), channel_id=1, replica_groups=mesh['ref'=2,'lines'=8,'cells'=8] {'lines','cells'}, dimensions={0} | all-to-all | bytes 786432 | tf_op jit(solution)/shard_map/all_to_all | solution.py:370
  59.4 0.4 right_side.1
  59.8 16.6 %all_to_all.41.recv = bf16[64,32,128]{2,1,0:T(8,128)(2,1)S(1)} all-to-all(bf16[64,32,128]{2,1,0:T(8,128)(2,1)S(1)} %get-tuple-element.39), channel_id=1, replica_groups=mesh['ref'=2,'lines'=8,'cells'=8] {'lines','cells'}, dimensions={0} | all-to-all | bytes 1048576 | tf_op jit(solution)/shard_map/all_to_all | solution.py:370
  76.4 0.0 copy-done
  76.4 0.0 copy-done.1
  76.4 0.0 copy-done.2
  76.4 0.0 copy-done.4
  76.4 6.1 %step.3 = (bf16[64,24,128]{2,1,0:T(8,128)(2,1)S(1)}, f32[32,128]{1,0:T(8,128)S(1)}, f32[32,128]{1,0:T(8,128)S(1)}, f32[8,128]{1,0:T(8,128)S(1)}, f32[2048,128]{1,0:T(8,128)S(1)}) custom-call(s32[512]{0:T(512)S(1)} %copy-done.3, s32[512]{0:T(512)S(1)} %multiply_add_fusion.slots, s32[1]{0:T(128)} %bitcast.me, ...), custom_call_target="tpu_custom_call" | custom-call | tf_op jit(solution)/shard_map/step/pallas_call | solution.py:420
  82.5 15.8 %all_to_all.42.recv = bf16[64,24,128]{2,1,0:T(8,128)(2,1)S(1)} all-to-all(bf16[64,24,128]{2,1,0:T(8,128)(2,1)S(1)} %get-tuple-element.41), channel_id=1, replica_groups=mesh['ref'=2,'lines'=8,'cells'=8] {'lines','cells'}, dimensions={0} | all-to-all | bytes 786432 | tf_op jit(solution)/shard_map/all_to_all | solution.py:370
  98.3 0.3 update.3
  98.7 16.6 %all_to_all.43.recv = bf16[64,32,128]{2,1,0:T(8,128)(2,1)S(1)} all-to-all(bf16[64,32,128]{2,1,0:T(8,128)(2,1)S(1)} %get-tuple-element.46), channel_id=1, replica_groups=mesh['ref'=2,'lines'=8,'cells'=8] {'lines','cells'}, dimensions={0} | all-to-all | bytes 1048576 | tf_op jit(solution)/shard_map/all_to_all | solution.py:370
  115.2 6.4 %step.4 = (bf16[64,24,128]{2,1,0:T(8,128)(2,1)S(1)}, f32[32,128]{1,0:T(8,128)S(1)}, f32[32,128]{1,0:T(8,128)S(1)}, f32[8,128]{1,0:T(8,128)S(1)}, f32[2048,128]{1,0:T(8,128)S(1)}) custom-call(s32[512]{0:T(512)S(1)} %copy-done.3, s32[512]{0:T(512)S(1)} %multiply_add_fusion.slots, s32[1]{0:T(128)} %bitcast.me, ...), custom_call_target="tpu_custom_call" | custom-call | tf_op jit(solution)/shard_map/step/pallas_call | solution.py:420
  121.6 15.8 %all_to_all.44.recv = bf16[64,24,128]{2,1,0:T(8,128)(2,1)S(1)} all-to-all(bf16[64,24,128]{2,1,0:T(8,128)(2,1)S(1)} %get-tuple-element.49), channel_id=1, replica_groups=mesh['ref'=2,'lines'=8,'cells'=8] {'lines','cells'}, dimensions={0} | all-to-all | bytes 786432 | tf_op jit(solution)/shard_map/all_to_all | solution.py:370
  137.4 0.3 update.4
  137.8 16.8 %all_to_all.45.recv = bf16[64,32,128]{2,1,0:T(8,128)(2,1)S(1)} all-to-all(bf16[64,32,128]{2,1,0:T(8,128)(2,1)S(1)} %get-tuple-element.54), channel_id=1, replica_groups=mesh['ref'=2,'lines'=8,'cells'=8] {'lines','cells'}, dimensions={0} | all-to-all | bytes 1048576 | tf_op jit(solution)/shard_map/all_to_all | solution.py:370
  154.6 6.4 %step.5 = (bf16[64,24,128]{2,1,0:T(8,128)(2,1)S(1)}, f32[32,128]{1,0:T(8,128)S(1)}, f32[32,128]{1,0:T(8,128)S(1)}, f32[8,128]{1,0:T(8,128)S(1)}) custom-call(s32[512]{0:T(512)S(1)} %copy-done.3, s32[512]{0:T(512)S(1)} %multiply_add_fusion.slots, s32[1]{0:T(128)} %bitcast.me, bf16[512,128,128]{2,1,0:T(8,128)(2,1)S(1)} %get-tuple-element.35.sens, ...), custom_call_target="tpu_custom_call" | custom-call | tf_op jit(solution)/shard_map/step/pallas_call | solution.py:420
  161.0 15.8 %all_to_all.46.recv = bf16[64,24,128]{2,1,0:T(8,128)(2,1)S(1)} all-to-all(bf16[64,24,128]{2,1,0:T(8,128)(2,1)S(1)} %get-tuple-element.57), channel_id=1, replica_groups=mesh['ref'=2,'lines'=8,'cells'=8] {'lines','cells'}, dimensions={0} | all-to-all | bytes 786432 | tf_op jit(solution)/shard_map/all_to_all | solution.py:370
  176.8 0.9 update.5
  (3 shorter events, 0.0 us)
Async XLA Ops:
  0.6 30.0 %copy-start.3 = (s32[512]{0:T(512)S(1)}, s32[512]{0:T(512)}, u32[]{:S(2)}) copy-start(s32[512]{0:T(512)} %cols.7) | copy-start | bytes 6148
  2.4 0.6 copy-start.5
  3.0 27.7 %all-to-all-start = ((bf16[64,48,128]{2,1,0:T(8,128)(2,1)}), bf16[64,48,128]{2,1,0:T(8,128)(2,1)S(1)}, u32[]{:S(2)}, u32[]{:S(2)}) async-start(bf16[64,48,128]{2,1,0:T(8,128)(2,1)} %get-tuple-element.33), calls=%async_computation | async-start | bytes 1572864 | tf_op jit(solution)/shard_map/all_to_all | solution.py:370
  43.5 32.9 %copy-start = (s32[1,6,32,128]{3,2,1,0:T(8,128)S(1)}, s32[1,6,32,128]{3,2,1,0:T(8,128)}, u32[]{:S(2)}) copy-start(s32[1,6,32,128]{3,2,1,0:T(8,128)} %copy.15) | copy-start | bytes 294916
  43.5 32.8 %copy-start.1 = (f32[4096]{0:T(1024)S(1)}, f32[4096]{0:T(1024)}, u32[]{:S(2)}) copy-start(f32[4096]{0:T(1024)} %param.15) | copy-start | bytes 49156
  43.5 32.8 %copy-start.2 = (f32[4096]{0:T(1024)S(1)}, f32[4096]{0:T(1024)}, u32[]{:S(2)}) copy-start(f32[4096]{0:T(1024)} %param.14) | copy-start | bytes 49156
  43.6 32.8 %copy-start.4 = (s32[512]{0:T(512)S(1)}, s32[512]{0:T(512)}, u32[]{:S(2)}) copy-start(s32[512]{0:T(512)} %param.10) | copy-start | bytes 6148
